TPU v7x, 32 devices: a whole 2x2x4 slice. The times are simulated.
32 devices in a mesh: gx: 4 (over y, x), gy: 8 (over z, core).
Axes of the slice: x: 2, y: 2, z: 4, core: 2. Of those that a mesh axis runs over, the one named last changes fastest.
Arguments:
- adjoint_e: bfloat16 [3, 128, 512, 128], P(None, 'gx', 'gy'), may hold values from -6 to 6
- adjoint_h: bfloat16 [3, 128, 512, 128], P(None, 'gx', 'gy'), may hold values from -6 to 6
- material: int32 [128, 512, 128], P('gx', 'gy'), may hold values from 0 to 3
- inv_eps: float32 [4], replicated, may hold values from 0.08 to 1
- forward_design: bfloat16 [3, 128, 512, 128], P(None, 'gx', 'gy'), may hold values from -6 to 6
- cell_slot: int32 [128, 512], P('gx', 'gy'), may hold values from 0 to 511, as said below
- tile_pillars: int32 [4, 8, 512], replicated, may hold values from -1 to 16383, as said below
- pillar_rank: int32 [16384], replicated, may hold values from 0 to 16383, as said below
Outputs:
- new_e: bfloat16 [3, 128, 512, 128], P(None, 'gx', 'gy')
- new_h: bfloat16 [3, 128, 512, 128], P(None, 'gx', 'gy')
- gradient: float32 [32, 16384], P(None, ('gx', 'gy'))
Inputs may be any that keep to these rules, and one draw needn't show every extreme that they name: `cell_slot`: the cell's slot holds the id of the pillar that covers the cell. `tile_pillars`: pillars are rectangles of 2 or 3 cells along x and along y that tile the lateral grid and never cross a tile's border. The lx-th pillar along x and ly-th along y of tile (tx, ty), counted from the tile's low corner, has id (tx * 16 + lx) * 256 + ty * 32 + ly. Each tile lists every pillar in it exactly once, in no particular order, with -1 in unused slots; tile (0, 0) uses all 512 slots. `pillar_rank`: A permutation of the pillar ids; rank r is owned by device r // 512 of gx+gy. Of the 512 ids of one tile, exactly 16 have ranks owned by each device.
All inputs are finite; a program needn't handle non-finite values.
Results may differ from a plain program's by a relative error of at most 0.0049.
Values may be sent and summed in bfloat16 or wider, within the bound.
A program may use at most 128 MiB of HBM per device.

v0:
```python
import jax
import jax.numpy as jnp
from jax import lax
from jax.sharding import PartitionSpec as P

DL = 32


courant = 0.5
grad_scale = 0.125


def shifted(block, axis, distance):
    devices = range(lax.axis_size(axis))
    route = [(i - distance, i) for i in devices if i - distance in devices]
    return lax.ppermute(block, axis, route)


def next_cell(field, axis):
    rest = lax.slice_in_dim(field, 1, field.shape[axis], axis=axis)
    edge = jnp.zeros_like(lax.slice_in_dim(field, 0, 1, axis=axis))
    return jnp.concatenate([rest, edge], axis=axis)


def prior_cell(field, axis):
    rest = lax.slice_in_dim(field, 0, field.shape[axis] - 1, axis=axis)
    edge = jnp.zeros_like(lax.slice_in_dim(field, 0, 1, axis=axis))
    return jnp.concatenate([edge, rest], axis=axis)


def join_next(field, face, axis):
    rest = lax.slice_in_dim(field, 1, field.shape[axis], axis=axis)
    return jnp.concatenate([rest, jnp.expand_dims(face.astype(jnp.float32), axis)], axis=axis)


def join_prior(field, face, axis):
    rest = lax.slice_in_dim(field, 0, field.shape[axis] - 1, axis=axis)
    return jnp.concatenate([jnp.expand_dims(face.astype(jnp.float32), axis), rest], axis=axis)


def material_coefficient(material, inv_eps):
    coefficient = jnp.zeros(material.shape, jnp.float32)
    for which in range(inv_eps.shape[0]):
        coefficient = coefficient + jnp.where(
            material == which, inv_eps[which], jnp.zeros((), jnp.float32)
        )
    return courant * coefficient


def per_device(
    adjoint_e, adjoint_h, material, inv_eps, forward_design, cell_slot, tile_pillars, pillar_rank
):
    slot_count = tile_pillars.shape[2]
    total_pillars = pillar_rank.shape[0]
    count_x = lax.axis_size("gx")
    count_y = lax.axis_size("gy")
    devices = count_x * count_y
    owned = total_pillars // devices
    gx_index = lax.axis_index("gx")
    gy_index = lax.axis_index("gy")
    device_index = gx_index * count_y + gy_index
    design_depth = forward_design.shape[3]
    slab = adjoint_e.astype(jnp.float32)
    intersection_density = jnp.sum(slab * forward_design.astype(jnp.float32), axis=0)
    cells_x, cells_y = cell_slot.shape
    layer_sums = intersection_density.reshape(cells_x * cells_y, DL, design_depth // DL).sum(axis=2)
    one_hot = (
        cell_slot.reshape(-1)[:, None] == jnp.arange(slot_count, dtype=jnp.int32)[None, :]
    ).astype(jnp.float32)
    partial_value = grad_scale * jnp.einsum(
        "cl,cs->ls",
        layer_sums,
        one_hot,
        precision=lax.Precision.HIGHEST,
        preferred_element_type=jnp.float32,
    )
    all_ranks = jnp.where(tile_pillars >= 0, pillar_rank[jnp.maximum(tile_pillars, 0)], -1)
    flat_ranks = all_ranks.reshape(-1, slot_count)
    first_owned = device_index * owned
    owned_ranks = first_owned + jnp.arange(owned, dtype=jnp.int32)
    empty = jnp.zeros((DL, owned), jnp.float32)
    pieces = lax.all_gather(partial_value[None], ("gx", "gy"), axis=0, tiled=True)

    def add_tile(offset_row, carried):
        slot_ranks = lax.dynamic_index_in_dim(flat_ranks, offset_row, 0, keepdims=False)
        selector = (slot_ranks[:, None] == owned_ranks[None, :]).astype(jnp.float32)
        tile_terms = lax.dynamic_index_in_dim(pieces, offset_row, 0, keepdims=False)
        return carried + jnp.dot(
            tile_terms,
            selector,
            precision=lax.Precision.HIGHEST,
            preferred_element_type=jnp.float32,
        )

    gradient = lax.fori_loop(0, pieces.shape[0], add_tile, empty)
    faces_x = shifted((adjoint_e[1, 0], adjoint_e[2, 0]), "gx", -1)
    faces_y = shifted((adjoint_e[0, :, 0], adjoint_e[2, :, 0]), "gy", -1)
    efield_x = adjoint_e[0].astype(jnp.float32)
    efield_y = adjoint_e[1].astype(jnp.float32)
    efield_z = adjoint_e[2].astype(jnp.float32)
    hnew_x = adjoint_h[0].astype(jnp.float32) - courant * (
        join_next(efield_z, faces_y[1], 1) - efield_z - (next_cell(efield_y, 2) - efield_y)
    )
    hnew_y = adjoint_h[1].astype(jnp.float32) - courant * (
        next_cell(efield_x, 2) - efield_x - (join_next(efield_z, faces_x[1], 0) - efield_z)
    )
    hnew_z = adjoint_h[2].astype(jnp.float32) - courant * (
        join_next(efield_y, faces_x[0], 0)
        - efield_y
        - (join_next(efield_x, faces_y[0], 1) - efield_x)
    )
    new_h = jnp.stack([hnew_x, hnew_y, hnew_z]).astype(jnp.bfloat16)
    back_x = shifted((new_h[1, -1], new_h[2, -1]), "gx", 1)
    back_y = shifted((new_h[0, :, -1], new_h[2, :, -1]), "gy", 1)
    magnetic_x = new_h[0].astype(jnp.float32)
    magnetic_y = new_h[1].astype(jnp.float32)
    magnetic_z = new_h[2].astype(jnp.float32)
    coefficient = material_coefficient(material, inv_eps)
    enew_x = efield_x + coefficient * (
        magnetic_z - join_prior(magnetic_z, back_y[1], 1) - (magnetic_y - prior_cell(magnetic_y, 2))
    )
    enew_y = efield_y + coefficient * (
        magnetic_x - prior_cell(magnetic_x, 2) - (magnetic_z - join_prior(magnetic_z, back_x[1], 0))
    )
    enew_z = efield_z + coefficient * (
        magnetic_y
        - join_prior(magnetic_y, back_x[0], 0)
        - (magnetic_x - join_prior(magnetic_x, back_y[0], 1))
    )
    new_e = jnp.stack([enew_x, enew_y, enew_z]).astype(jnp.bfloat16)
    return (new_e, new_h, gradient)


def solution(mesh):
    return jax.shard_map(
        per_device,
        mesh=mesh,
        in_specs=(
            P(None, "gx", "gy", None),
            P(None, "gx", "gy", None),
            P("gx", "gy", None),
            P(),
            P(None, "gx", "gy", None),
            P("gx", "gy"),
            P(),
            P(),
        ),
        out_specs=(P(None, "gx", "gy", None), P(None, "gx", "gy", None), P(None, ("gx", "gy"))),
        check_vma=False,
    )
```

profile of v0, /device:TPU:0, one launch (start us, length us, event | category | flops | bytes accessed | tf_op | source)
XLA Modules:
  0.0 220.6 jit_solution(7150098035155643632)
XLA Ops:
  8.0 1.3 collective-permute-start.3
  9.3 0.9 fusion.44
  10.2 1.3 collective-permute-start.4
  11.5 1.3 collective-permute-start
  12.8 1.3 collective-permute-start.1
  14.1 2.6 %multiply_reduce_fusion = f32[32,64,128]{2,1,0:T(8,128)S(1)} fusion(bf16[3,32,64,128]{3,2,1,0:T(8,128)(2,1)} %param.14, bf16[3,32,64,128]{3,2,1,0:T(8,128)(2,1)} %param.10), kind=kLoop, calls=%fused_computation.13 | loop fusion | flops 2883584 | bytes 4194304 | tf_op jit(solution)/shard_map/reduce_sum | solution.py:64
  16.7 1.8 copy.59
  18.5 1.8 reshape.42
  20.4 2.0 reduce_sum.19
  22.4 2.2 %fusion.10 = f32[32,512]{1,0:T(8,128)} fusion(f32[2048,32]{0,1:T(8,128)S(1)} %reduce_sum.19, s32[2048]{0:T(1024)S(1)} %eq.84), kind=kOutput, calls=%fused_computation.19 | convolution fusion | flops 403718144 | bytes 335872 | tf_op jit(solution)/shard_map/cl,cs->ls/dot_general | solution.py:70
  24.8 2.0 copy_convert_fusion
  26.8 1.1 slice_bitcast_fusion.2
  28.6 1.1 fusion.43
  29.8 1.0 slice_bitcast_fusion.3
  30.8 90.5 %gather_fusion = s32[16384]{0:T(1024)S(1)} fusion(s32[16384]{0:T(1024)S(1)} %copy-done, s32[16384]{0:T(1024)S(1)} %broadcast_clamp_fusion), kind=kCustom, calls=%fused_computation | custom fusion | bytes 196608 | tf_op jit(solution)/shard_map/gather | solution.py:77
  122.0 1.4 slice.149
  123.4 1.6 slice.153
  125.0 2.2 %slice.152 = f32[32,63,128]{2,0,1:T(8,128)} slice(f32[32,64,128]{2,0,1:T(8,128)} %get-tuple-element.163), slice={[0:32], [1:64], [0:128]} | slice | bytes 2064384 | tf_op jit(solution)/shard_map/slice | solution.py:32
  127.3 1.1 slice.145
  128.5 2.9 %convert_bitcast_fusion.2 = (f32[32,64,128]{2,0,1:T(8,128)S(1)}, bf16[1,32,64,128]{3,1,2,0:T(8,128)(2,1)S(1)}) fusion(bf16[1,32,64,128]{3,2,1,0:T(8,128)(2,1)S(1)} %get-tuple-element.151, f32[1,32,1,128]{3,1,2,0:T(8,128)S(1)} %bitcast_convert_fusion.3, f32[1,32,63,128]{3,1,2,0:T(8,128)} %slice_bitcast_fusion.3, ...), kind=kLoop, calls=%fused_computation.66 | loop fusion | flops 3145728 | bytes 5242880 | tf_op jit(solution)/shard_map/convert_element_type | solution.py:117
  131.6 1.0 copy-done.3
  132.7 2.0 convert_bitcast_fusion.1
  135.1 1.8 copy.61
  136.9 6.1 %collective-permute-start.5 = (bf16[64,128]{1,0:T(8,128)(2,1)S(1)}, bf16[64,128]{1,0:T(8,128)(2,1)S(1)}, u32[]{:S(2)}, u32[]{:S(2)}) collective-permute-start(bf16[64,128]{1,0:T(8,128)(2,1)S(1)} %bitcast.136), channel_id=1, source_target_pairs={{0,8},{8,16},{16,24},{1,9},{9,17},{17,25},{2,10},{10,18},{18,26},{... | collective-permute-start | bytes 49160 | tf_op jit(solution)/shard_map/ppermute | solution.py:16
  143.0 3.4 %collective-permute-start.2 = (bf16[32,128]{1,0:T(8,128)(2,1)S(1)}, bf16[32,128]{1,0:T(8,128)(2,1)S(1)}, u32[]{:S(2)}, u32[]{:S(2)}) collective-permute-start(bf16[32,128]{1,0:T(8,128)(2,1)S(1)} %slice_bitcast_fusion.7), channel_id=1, source_target_pairs={{0,1},{1,2},{2,3},{3,4},{4,5},{5,6},{6,7},{8,9},{9,10},{10,11},{11... | collective-permute-start | bytes 24584 | tf_op jit(solution)/shard_map/ppermute | solution.py:16
  146.5 3.9 %collective-permute-start.7 = (bf16[32,128]{1,0:T(8,128)(2,1)S(1)}, bf16[32,128]{1,0:T(8,128)(2,1)S(1)}, u32[]{:S(2)}, u32[]{:S(2)}) collective-permute-start(bf16[32,128]{1,0:T(8,128)(2,1)S(1)} %slice_bitcast_fusion.6), channel_id=1, source_target_pairs={{0,1},{1,2},{2,3},{3,4},{4,5},{5,6},{6,7},{8,9},{9,10},{10,11},{11... | collective-permute-start | bytes 24584 | tf_op jit(solution)/shard_map/ppermute | solution.py:16
  150.8 5.0 %collective-permute-start.6 = (bf16[64,128]{1,0:T(8,128)(2,1)S(1)}, bf16[64,128]{1,0:T(8,128)(2,1)S(1)}, u32[]{:S(2)}, u32[]{:S(2)}) collective-permute-start(bf16[64,128]{1,0:T(8,128)(2,1)S(1)} %bitcast.137), channel_id=1, source_target_pairs={{0,8},{8,16},{16,24},{1,9},{9,17},{17,25},{2,10},{10,18},{18,26},{... | collective-permute-start | bytes 49160 | tf_op jit(solution)/shard_map/ppermute | solution.py:16
  155.8 1.4 collective-permute-done.6
  157.2 3.9 %fusion.38 = bf16[1,32,64,128]{3,1,2,0:T(8,128)(2,1)S(1)} fusion(f32[32,63,128]{2,0,1:T(8,128)S(1)} %slice.160, f32[32,1,128]{2,0,1:T(8,128)S(1)} %bitcast_convert_fusion, bf16[32,64,128]{2,0,1:T(8,128)(2,1)S(1)} %get-tuple-element.156, f32[31,64,128]{2,0,1:T(8,128)S(1)} %slice_bitcast_fusion, f32[1,64,128]{2,0,1:T(1,128)S(1)} %bitcast.134, ...), kind=kLoop, calls=%fused_computation.63 | loop fusion | flops 6029312 | bytes 5242896 | tf_op jit(solution)/shard_map/stack | solution.py:130
  161.1 4.4 %fusion.36 = (bf16[1,32,64,128]{3,1,2,0:T(8,128)(2,1)S(1)}, bf16[1,32,64,128]{3,1,2,0:T(8,128)(2,1)S(1)}) fusion(f32[32,64,127]{2,0,1:T(8,128)S(1)} %bitcast.129, f32[32,63,128]{2,0,1:T(8,128)S(1)} %slice.148, f32[32,1,128]{2,0,1:T(8,128)S(1)} %bitcast_convert_fusion.2, bf16[1,32,64,128]{3,2,1,0:T(8,128)(2,1)S(1)} %get-tuple-element.151, ...), kind=kLoop, calls=%fused_computation.61 | loop fusion | flops 8126464 | bytes 8896528 | tf_op jit(solution)/shard_map/stack | solution.py:130
  165.7 1.8 copy.60
  167.4 45.7 %while.14 = (s32[]{:T(128)}, f32[32,512]{1,0:T(8,128)S(1)}, f32[32,32,512]{2,1,0:T(8,128)}, s32[32,512]{1,0:T(8,128)S(1)}, s32[]{:T(128)}, /*index=5*/s32[]{:T(128)}, s32[]{:T(128)}) while((s32[]{:T(128)}, f32[32,512]{1,0:T(8,128)S(1)}, f32[32,32,512]{2,1,0:T(8,128)}, s32[32,512]{1,0:T(8,128)S(1)}, s32[]{:T(128)}, ...), condition=%wide.region_3.4_spmd.clone, body=%wide.region_2.3_spmd.clone.sunk | while | flops 100958720 | bytes 207455 | solution.py:95
  167.5 1.4 convolution_add_fusion.2
  168.9 1.4 convolution_add_fusion.2
  170.3 1.4 convolution_add_fusion.2
  171.8 1.4 convolution_add_fusion.2
  173.2 1.4 convolution_add_fusion.2
  174.6 1.4 convolution_add_fusion.2
  176.0 1.4 convolution_add_fusion.2
  177.5 1.4 convolution_add_fusion.2
  178.9 1.4 convolution_add_fusion.2
  180.3 1.4 convolution_add_fusion.2
  181.8 1.4 convolution_add_fusion.2
  183.2 1.4 convolution_add_fusion.2
  184.6 1.4 convolution_add_fusion.2
  186.0 1.4 convolution_add_fusion.2
  187.5 1.4 convolution_add_fusion.2
  188.9 1.4 convolution_add_fusion.2
  190.3 1.4 convolution_add_fusion.2
  191.8 1.4 convolution_add_fusion.2
  193.2 1.4 convolution_add_fusion.2
  194.6 1.4 convolution_add_fusion.2
  196.0 1.4 convolution_add_fusion.2
  197.5 1.4 convolution_add_fusion.2
  198.9 1.4 convolution_add_fusion.2
  200.3 1.4 convolution_add_fusion.2
  201.8 1.4 convolution_add_fusion.2
  203.2 1.4 convolution_add_fusion.2
  204.6 1.4 convolution_add_fusion.2
  206.0 1.4 convolution_add_fusion.2
  207.5 1.4 convolution_add_fusion.2
  208.9 1.4 convolution_add_fusion.2
  210.3 1.4 convolution_add_fusion.2
  211.8 1.4 convolution_add_fusion.2
  (135 shorter events, 4.9 us)
Async XLA Ops:
  7.2 23.6 %copy-start = (s32[16384]{0:T(1024)S(1)}, s32[16384]{0:T(1024)}, u32[]{:S(2)}) copy-start(s32[16384]{0:T(1024)} %param.17) | copy-start | bytes 196612
  7.2 160.3 %all-gather.3.cloned.1.call-start = ((), (), s32[]{:S(2)}) async-start(), calls=%async_computation | async-start | bytes 2162688 | tf_op jit(solution)/shard_map/all_gather | solution.py:82
  8.0 123.6 %collective-permute-start.3 = (bf16[64,128]{1,0:T(8,128)(2,1)S(1)}, bf16[64,128]{1,0:T(8,128)(2,1)S(1)}, u32[]{:S(2)}, u32[]{:S(2)}) collective-permute-start(bf16[64,128]{1,0:T(8,128)(2,1)S(1)} %get-tuple-element.148), channel_id=1, source_target_pairs={{8,0},{16,8},{24,16},{9,1},{17,9},{25,17},{10,2},{18,10},{26,18},{... | collective-permute-start | bytes 49160 | tf_op jit(solution)/shard_map/ppermute | solution.py:16
  10.2 118.2 %collective-permute-start.4 = (bf16[32,128]{1,0:T(8,128)(2,1)S(1)}, bf16[32,128]{1,0:T(8,128)(2,1)S(1)}, u32[]{:S(2)}, u32[]{:S(2)}) collective-permute-start(bf16[32,128]{1,0:T(8,128)(2,1)S(1)} %bitcast.138), channel_id=1, source_target_pairs={{1,0},{2,1},{3,2},{4,3},{5,4},{6,5},{7,6},{9,8},{10,9},{11,10},{12... | collective-permute-start | bytes 24584 | tf_op jit(solution)/shard_map/ppermute | solution.py:16
  11.5 116.9 %collective-permute-start = (bf16[64,128]{1,0:T(8,128)(2,1)S(1)}, bf16[64,128]{1,0:T(8,128)(2,1)S(1)}, u32[]{:S(2)}, u32[]{:S(2)}) collective-permute-start(bf16[64,128]{1,0:T(8,128)(2,1)S(1)} %get-tuple-element.147), channel_id=1, source_target_pairs={{8,0},{16,8},{24,16},{9,1},{17,9},{25,17},{10,2},{18,10},{26,18},{... | collective-permute-start | bytes 49160 | tf_op jit(solution)/shard_map/ppermute | solution.py:16
  12.8 115.6 %collective-permute-start.1 = (bf16[32,128]{1,0:T(8,128)(2,1)S(1)}, bf16[32,128]{1,0:T(8,128)(2,1)S(1)}, u32[]{:S(2)}, u32[]{:S(2)}) collective-permute-start(bf16[32,128]{1,0:T(8,128)(2,1)S(1)} %bitcast.139), channel_id=1, source_target_pairs={{1,0},{2,1},{3,2},{4,3},{5,4},{6,5},{7,6},{9,8},{10,9},{11,10},{12... | collective-permute-start | bytes 24584 | tf_op jit(solution)/shard_map/ppermute | solution.py:16
  18.5 1.8 copy-start.10
  20.3 4.3 %copy-start.1 = (bf16[3,32,64,128]{3,2,1,0:T(8,128)(2,1)S(1)}, bf16[3,32,64,128]{3,2,1,0:T(8,128)(2,1)}, u32[]{:S(2)}) copy-start(bf16[3,32,64,128]{3,2,1,0:T(8,128)(2,1)} %param.10) | copy-start | bytes 4718596
  26.8 1.8 copy-start.8
  28.6 1.1 copy-start.9
  30.8 90.6 %copy-start.11 = (f32[4]{0:T(128)S(1)}, f32[4]{0:T(128)}, u32[]{:S(2)}) copy-start(f32[4]{0:T(128)} %param.13) | copy-start | bytes 52
  123.4 3.9 %copy-start.5 = (f32[1,32,64,128]{3,1,2,0:T(8,128)S(1)}, f32[1,32,64,128]{3,1,2,0:T(8,128)}, u32[]{:S(2)}) copy-start(f32[1,32,64,128]{3,1,2,0:T(8,128)} %get-tuple-element.154) | copy-start | bytes 3145732
  128.4 3.1 %copy-start.4 = (f32[32,64,127]{2,0,1:T(8,128)S(1)}, f32[32,64,127]{2,0,1:T(8,128)}, u32[]{:S(2)}) copy-start(f32[32,64,127]{2,0,1:T(8,128)} %slice.149) | copy-start | bytes 3121156
  128.4 3.1 %copy-start.6 = (f32[32,63,128]{2,0,1:T(8,128)S(1)}, f32[32,63,128]{2,0,1:T(8,128)}, u32[]{:S(2)}) copy-start(f32[32,63,128]{2,0,1:T(8,128)} %slice.152) | copy-start | bytes 3096580
  131.3 1.2 copy-start.3
  131.3 1.3 copy-start.7
  136.9 18.9 %collective-permute-start.5 = (bf16[64,128]{1,0:T(8,128)(2,1)S(1)}, bf16[64,128]{1,0:T(8,128)(2,1)S(1)}, u32[]{:S(2)}, u32[]{:S(2)}) collective-permute-start(bf16[64,128]{1,0:T(8,128)(2,1)S(1)} %bitcast.136), channel_id=1, source_target_pairs={{0,8},{8,16},{16,24},{1,9},{9,17},{17,25},{2,10},{10,18},{18,26},{... | collective-permute-start | bytes 49160 | tf_op jit(solution)/shard_map/ppermute | solution.py:16
  143.0 12.7 %collective-permute-start.2 = (bf16[32,128]{1,0:T(8,128)(2,1)S(1)}, bf16[32,128]{1,0:T(8,128)(2,1)S(1)}, u32[]{:S(2)}, u32[]{:S(2)}) collective-permute-start(bf16[32,128]{1,0:T(8,128)(2,1)S(1)} %slice_bitcast_fusion.7), channel_id=1, source_target_pairs={{0,1},{1,2},{2,3},{3,4},{4,5},{5,6},{6,7},{8,9},{9,10},{10,11},{11... | collective-permute-start | bytes 24584 | tf_op jit(solution)/shard_map/ppermute | solution.py:16
  146.5 9.3 %collective-permute-start.7 = (bf16[32,128]{1,0:T(8,128)(2,1)S(1)}, bf16[32,128]{1,0:T(8,128)(2,1)S(1)}, u32[]{:S(2)}, u32[]{:S(2)}) collective-permute-start(bf16[32,128]{1,0:T(8,128)(2,1)S(1)} %slice_bitcast_fusion.6), channel_id=1, source_target_pairs={{0,1},{1,2},{2,3},{3,4},{4,5},{5,6},{6,7},{8,9},{9,10},{10,11},{11... | collective-permute-start | bytes 24584 | tf_op jit(solution)/shard_map/ppermute | solution.py:16
  150.6 6.6 %copy-start.2 = (s32[32,64,128]{2,1,0:T(8,128)S(1)}, s32[32,64,128]{2,1,0:T(8,128)}, u32[]{:S(2)}) copy-start(s32[32,64,128]{2,1,0:T(8,128)} %param.12) | copy-start | bytes 3145732
  150.8 6.4 %collective-permute-start.6 = (bf16[64,128]{1,0:T(8,128)(2,1)S(1)}, bf16[64,128]{1,0:T(8,128)(2,1)S(1)}, u32[]{:S(2)}, u32[]{:S(2)}) collective-permute-start(bf16[64,128]{1,0:T(8,128)(2,1)S(1)} %bitcast.137), channel_id=1, source_target_pairs={{0,8},{8,16},{16,24},{1,9},{9,17},{17,25},{2,10},{10,18},{18,26},{... | collective-permute-start | bytes 49160 | tf_op jit(solution)/shard_map/ppermute | solution.py:16
  213.1 0.6 copy-start.12
Sparse Core Ops, SparseCore 0:
  24.8 63.9 all-gather.2
where the time goes:
time: 223 us; the launch traced here: 221 us
  local copies, waits for them, and re-layouts  113 us (51%)
  matrix products  46 us (21%)
  starting transfers between devices  23.5 us (11%)
  other arithmetic  21 us (9%)
  between operations  14.5 us (7%)
    gather x2, local copies, waits for them, and re-layouts, per_device(): pillar_rank[jnp.maximum(tile_pillars, 0)]  90.5 us
    dot_general x32, matrix products, add_tile(): jnp.dot(tile_terms, selector, precision=lax.Precision.HIGHEST, preferred_...  43.8 us
    ppermute x8, starting transfers between devices, shifted(): return lax.ppermute(block, axis, route)  23.5 us
    another operation x3, other arithmetic, per_device(): new_e = jnp.stack([enew_x, enew_y, enew_z]).astype(jnp.bfloat16)  8.51 us
    unnamed x33, local copies, waits for them, and re-layouts  5.68 us
    slice x3, local copies, waits for them, and re-layouts, join_next(): rest = lax.slice_in_dim(field, 1, field.shape[axis], axis=axis)  4.5 us
  transfers between devices with their start and end apart: 9, of which 1 were waited for; matrix products, arithmetic and copies ran while one was open for 60% of the time, Pallas kernels for 0%

commit v1 on v0

v1 whole, which is shorter than its diff:
```python
import functools

import jax
import jax.numpy as jnp
from jax import lax
from jax.experimental import pallas as pl
from jax.experimental.pallas import tpu as pltpu
from jax.sharding import PartitionSpec as P

DL = 32

courant = 0.5
grad_scale = 0.125

MESH = pl.DeviceIdType.MESH
f32 = jnp.float32
bf16 = jnp.bfloat16
LANES = 128
BLOCK = 8


def iota(shape, axis):
    return lax.broadcasted_iota(jnp.int32, shape, axis)


def dot(a, b):
    return jnp.dot(a, b, preferred_element_type=f32)


def one_hot(mask):
    return jnp.where(mask, 1.0, 0.0).astype(bf16)


def split(value):
    high = value.astype(bf16)
    return high, (value - high.astype(f32)).astype(bf16)


def kernel(
    count_x,
    count_y,
    e_hbm,
    h_hbm,
    m_hbm,
    eps,
    f_hbm,
    cs_hbm,
    tp_hbm,
    pr_hbm,
    ne,
    nh,
    grad,
    e_v,
    h_v,
    m_v,
    f_v,
    cs_v,
    tp_v,
    pr_v,
    rt_v,
    acc,
    stage,
    out_y_prev,
    out_y_next,
    in_xn,
    in_xpe,
    in_xph,
    in_yn,
    in_yp,
    in_c1,
    in_c2,
    yn,
    hy_edge,
    send,
    recv,
    load_sem,
    face_send,
    face_recv,
    part_send,
    part_recv,
):
    _, cx, cy, nz = e_hbm.shape
    slots = tp_hbm.shape[2]
    devices = count_x * count_y
    half_x, half_y = cx // 2, cy // 2
    width = count_y * half_y
    rank_rows = pr_v.shape[0]
    per_device = slots // devices
    groups = LANES // DL
    rows = per_device // groups
    owned = pr_hbm.shape[0] * LANES // devices

    gx, gy = lax.axis_index("gx"), lax.axis_index("gy")
    me = gx * count_y + gy

    loads = [
        pltpu.make_async_copy(src, dst, load_sem.at[i])
        for i, (src, dst) in enumerate(
            [
                (e_hbm, e_v.at[:, pl.ds(0, cx)]),
                (h_hbm, h_v),
                (tp_hbm.at[gx], tp_v),
                (pr_hbm.at[pl.ds(pl.multiple_of(gx * rank_rows, 8), rank_rows)], pr_v),
                (cs_hbm, cs_v),
                (f_hbm, f_v),
                (m_hbm, m_v),
            ]
        )
    ]
    for load in loads:
        load.start()

    barrier = pltpu.get_barrier_semaphore()

    def partner(step):
        device = lax.rem(me + step, devices)
        return device, (lax.div(device, count_y), lax.rem(device, count_y))

    def greet(step, carry):
        pl.semaphore_signal(barrier, inc=1, device_id=partner(step)[1], device_id_type=MESH)
        return carry

    lax.fori_loop(1, devices, greet, 0)

    loads[0].wait()
    loads[1].wait()

    def gather_rows(x, carry):
        for c in range(3):
            first = e_v[c, x, 0:16, :].astype(f32)
            last = e_v[c, x, cy - 16 : cy, :].astype(f32)
            stage[c, pl.ds(x, 1), :] = first[0:1]
            stage[3 + c, pl.ds(x, 1), :] = last[15:16]
        for k, c in enumerate((0, 2)):
            stage[6 + k, pl.ds(x, 1), :] = h_v[c, x, cy - 16 : cy, :].astype(f32)[15:16]
        return carry

    lax.fori_loop(0, cx, gather_rows, 0)
    out_y_prev[0] = stage[0].astype(bf16)
    out_y_prev[1] = stage[2].astype(bf16)
    for k in range(5):
        out_y_next[k] = stage[3 + k].astype(bf16)

    pl.semaphore_wait(barrier, devices - 1)

    faces = [
        (e_hbm.at[pl.ds(1, 2), 0], in_xn, -1, 0),
        (out_y_prev, in_yn, 0, -1),
        (e_hbm.at[:, cx - 1], in_xpe, 1, 0),
        (h_hbm.at[pl.ds(1, 2), cx - 1], in_xph, 1, 0),
        (out_y_next, in_yp, 0, 1),
        (e_hbm.at[0, cx - 1, pl.ds(0, 16)], in_c1, 1, -1),
        (e_hbm.at[1, 0, pl.ds(cy - 16, 16)], in_c2, -1, 1),
    ]

    def inside(step_x, step_y):
        there = None
        for at, step, count in ((gx, step_x, count_x), (gy, step_y, count_y)):
            if step:
                fits = at + step < count if step > 0 else at + step >= 0
                there = fits if there is None else jnp.logical_and(there, fits)
        return there

    def face_copy(i):
        source, landing, step_x, step_y = faces[i]
        return pltpu.make_async_remote_copy(
            src_ref=source,
            dst_ref=landing,
            send_sem=face_send.at[i],
            recv_sem=face_recv.at[i],
            device_id=(gx + step_x, gy + step_y),
            device_id_type=MESH,
        )

    for i, (_, landing, step_x, step_y) in enumerate(faces):

        @pl.when(inside(step_x, step_y))
        def _():
            face_copy(i).start()

        @pl.when(jnp.logical_not(inside(-step_x, -step_y)))
        def _():
            landing[...] = jnp.zeros(landing.shape, landing.dtype)

    loads[2].wait()
    loads[3].wait()
    tile_row = iota(tp_v.shape, 0) == gy
    ids = jnp.sum(jnp.where(tile_row, tp_v[...], 0), axis=0, keepdims=True)
    listed = ids >= 0
    local = jnp.where(listed, ids - gx * (half_x * width), 0)
    local_row, local_lane = lax.div(local, LANES), lax.rem(local, LANES)
    ranks = pr_v[...]
    if rank_rows < LANES:
        ranks = jnp.concatenate(
            [ranks, jnp.zeros((LANES - rank_rows, LANES), jnp.int32)], axis=0
        )
    turned_high = lax.shift_right_logical(ranks, 8).astype(f32).T
    turned_low = lax.bitwise_and(ranks, 255).astype(f32).T
    table = jnp.concatenate([turned_high.astype(bf16), turned_low.astype(bf16)], axis=0)
    picked = dot(table, one_hot(iota((LANES, slots), 0) == local_row))
    picked = 256.0 * picked[:LANES] + picked[LANES:]
    slot_rank = jnp.sum(
        jnp.where(iota((LANES, slots), 0) == local_lane, picked, 0.0), axis=0, keepdims=True
    )
    turned = 256.0 * turned_high + turned_low
    along_y = lax.rem(iota((LANES, LANES), 1) * LANES + iota((LANES, LANES), 0), width)
    rt_v[...] = jnp.where(lax.div(along_y, half_y) == gy, turned, 1e9)
    tile_ranks = rt_v[
        pl.ds(pl.multiple_of(lax.rem(gy * half_y, LANES), half_y), half_y), :
    ]
    below = jnp.zeros((half_y, slots), f32)
    for j in range(rank_rows):
        below = below + jnp.where(tile_ranks[:, j : j + 1] < slot_rank, 1.0, 0.0)
    place = jnp.sum(below, axis=0, keepdims=True).astype(jnp.int32)
    owner, nth = lax.div(place, per_device), lax.rem(place, per_device)
    line = lax.div(nth, rows) * LANES + lax.rem(nth, rows) * devices + owner
    line = jnp.where(listed, line, -1)
    chosen = iota((slots, slots), 0) == line
    order = one_hot(chosen)
    own_rank = lax.rem(slot_rank.astype(jnp.int32), owned).astype(f32)
    rank_lines = jnp.sum(jnp.where(chosen, own_rank, 0.0), axis=1, keepdims=True)
    lane_group = lax.div(iota((LANES, LANES), 1), DL)
    rank_block = jnp.zeros((LANES, LANES), f32)
    for j in range(groups):
        rank_block = jnp.where(
            lane_group == j, rank_lines[j * LANES : (j + 1) * LANES], rank_block
        )

    loads[4].wait()
    loads[5].wait()
    batch = 256 // cy

    def add_cells(g, carry):
        slot_parts, parts = [], []
        for a in range(batch):
            x = g * batch + a
            slot_parts.append(cs_v[pl.ds(x, 1), :])
            density = e_v[0, x].astype(f32) * f_v[0, x].astype(f32)
            for c in (1, 2):
                density = density + e_v[c, x].astype(f32) * f_v[c, x].astype(f32)
            parts.append(jnp.concatenate(split(density), axis=1))
        cell_slots = jnp.concatenate(slot_parts, axis=1)
        hot = one_hot(iota((slots, batch * cy), 0) == cell_slots)
        acc[...] += dot(hot, jnp.concatenate(parts, axis=0))
        return carry

    acc[...] = jnp.zeros_like(acc)
    lax.fori_loop(0, cx // batch, add_cells, 0)
    sums = acc[:, :nz] + acc[:, nz:]
    sorted_sums = dot(order, jnp.concatenate(split(sums), axis=1)).astype(bf16)
    packed = jnp.concatenate(
        [
            jnp.concatenate(
                [
                    sorted_sums[j * LANES : (j + 1) * LANES, half * nz : (half + 1) * nz]
                    for j in range(groups)
                ],
                axis=1,
            )
            for half in range(2)
        ],
        axis=0,
    )
    pool_row, pool_lane = iota((groups * nz, LANES), 0), iota((groups * nz, LANES), 1)
    pool_to = lax.div(pool_row, nz) * DL + lax.div(lax.rem(pool_row, nz), nz // DL)
    pooled = dot(packed, one_hot(pool_to == pool_lane))
    pooled = pooled[:LANES] + pooled[LANES:]
    if 2 * rows < BLOCK:
        send[...] = jnp.zeros_like(send)
    for i in range(rows):
        part = slice(i * devices, (i + 1) * devices)
        send[pl.ds(i, devices, stride=BLOCK), :] = pooled[part]
        send[pl.ds(rows + i, devices, stride=BLOCK), :] = rank_block[part]

    mine = pl.ds(pl.multiple_of(me * BLOCK, BLOCK), BLOCK)

    def send_part(step, carry):
        device, where = partner(step)
        pltpu.make_async_remote_copy(
            src_ref=send.at[pl.ds(pl.multiple_of(device * BLOCK, BLOCK), BLOCK)],
            dst_ref=recv.at[mine],
            send_sem=part_send,
            recv_sem=part_recv,
            device_id=where,
            device_id_type=MESH,
        ).start()
        return carry

    lax.fori_loop(1, devices, send_part, 0)
    recv[mine, :] = send[mine, :]

    for i, (_, _, step_x, step_y) in enumerate(faces):

        @pl.when(inside(-step_x, -step_y))
        def _():
            face_copy(i).wait_recv()

    for c in (1, 2):
        e_v[c, cx] = in_xn[c - 1]
    for k in range(2):
        yn[k] = in_yn[k].astype(f32)

    last_lane = iota((1, nz), 1) == nz - 1
    first_lane = iota((1, nz), 1) == 0

    def next_z(field):
        return jnp.where(last_lane, 0.0, pltpu.roll(field, nz - 1, 1))

    def prior_z(field):
        return jnp.where(first_lane, 0.0, pltpu.roll(field, 1, 1))

    def next_row(field, edge):
        size = field.shape[0]
        return jnp.where(
            iota((size, 1), 0) == size - 1, edge, pltpu.roll(field, size - 1, 0)
        )

    def prior_row(field, edge):
        return jnp.where(iota((field.shape[0], 1), 0) == 0, edge, pltpu.roll(field, 1, 0))

    pe_x, pe_y, pe_z, ph_x, ph_z = [in_yp[k].astype(f32) for k in range(5)]
    first_x, first_z = stage[0], stage[2]
    edge_x = ph_x - courant * ((first_z - pe_z) - (next_z(pe_y) - pe_y))
    corner = in_c2[...].astype(f32)[15:16]
    edge_z = ph_z - courant * ((next_row(pe_y, corner) - pe_y) - (first_x - pe_x))
    keep_y = gy > 0
    hy_edge[0] = jnp.where(keep_y, edge_x, 0.0).astype(bf16).astype(f32)
    hy_edge[1] = jnp.where(keep_y, edge_z, 0.0).astype(bf16).astype(f32)

    pe_x, pe_y, pe_z = [in_xpe[k].astype(f32) for k in range(3)]
    ph_y, ph_z = [in_xph[k].astype(f32) for k in range(2)]
    first_y, first_z = e_v[1, 0].astype(f32), e_v[2, 0].astype(f32)
    back_y = ph_y - courant * ((next_z(pe_x) - pe_x) - (first_z - pe_z))
    corner = in_c1[...].astype(f32)[0:1]
    back_z = ph_z - courant * ((first_y - pe_y) - (next_row(pe_x, corner) - pe_x))
    keep_x = gx > 0
    back_y = jnp.where(keep_x, back_y, 0.0).astype(bf16)
    back_z = jnp.where(keep_x, back_z, 0.0).astype(bf16)

    loads[6].wait()
    factors = [courant * eps[k] for k in range(eps.shape[0])]

    def update(x, carry):
        back_y, back_z = [value.astype(f32) for value in carry]
        e_x, e_y, e_z = [e_v[c, x].astype(f32) for c in range(3)]
        nx_y, nx_z = [e_v[c, x + 1].astype(f32) for c in (1, 2)]
        ny_x, ny_z = [yn[k, pl.ds(x, 1), :] for k in range(2)]
        d_y_z, d_z_y = next_row(e_z, ny_z) - e_z, next_z(e_y) - e_y
        h_x = (h_v[0, x].astype(f32) - courant * (d_y_z - d_z_y)).astype(bf16)
        d_z_x, d_x_z = next_z(e_x) - e_x, nx_z - e_z
        h_y = (h_v[1, x].astype(f32) - courant * (d_z_x - d_x_z)).astype(bf16)
        d_x_y, d_y_x = nx_y - e_y, next_row(e_x, ny_x) - e_x
        h_z = (h_v[2, x].astype(f32) - courant * (d_x_y - d_y_x)).astype(bf16)
        nh[0, x], nh[1, x], nh[2, x] = h_x, h_y, h_z
        ahead = (h_y, h_z)
        h_x, h_y, h_z = h_x.astype(f32), h_y.astype(f32), h_z.astype(f32)
        before_x, before_z = [hy_edge[k, pl.ds(x, 1), :] for k in range(2)]
        material = m_v[x]
        factor = jnp.full(material.shape, factors[-1], f32)
        for which in range(len(factors) - 1):
            factor = jnp.where(material == which, factors[which], factor)
        b_y_z, b_z_y = h_z - prior_row(h_z, before_z), h_y - prior_z(h_y)
        ne[0, x] = (e_x + factor * (b_y_z - b_z_y)).astype(bf16)
        b_z_x, b_x_z = h_x - prior_z(h_x), h_z - back_z
        ne[1, x] = (e_y + factor * (b_z_x - b_x_z)).astype(bf16)
        b_x_y, b_y_x = h_y - back_y, h_x - prior_row(h_x, before_x)
        ne[2, x] = (e_z + factor * (b_x_y - b_y_x)).astype(bf16)
        return ahead

    lax.fori_loop(0, cx, update, (back_y, back_z))

    others = pl.ds(0, (devices - 1) * BLOCK)
    arrivals = pltpu.make_async_remote_copy(
        src_ref=send.at[others],
        dst_ref=recv.at[others],
        send_sem=part_send,
        recv_sem=part_recv,
        device_id=(gx, gy),
        device_id_type=MESH,
    )
    arrivals.wait_recv()
    values = jnp.concatenate(
        [recv[pl.ds(i, devices, stride=BLOCK), :] for i in range(rows)], axis=0
    )
    value_ranks = jnp.concatenate(
        [recv[pl.ds(rows + i, devices, stride=BLOCK), :] for i in range(rows)], axis=0
    )
    turned_values = values.T
    terms = jnp.concatenate(
        [turned_values[j * DL : (j + 1) * DL] for j in range(groups)], axis=1
    )
    lane_rank = iota((LANES, owned), 1).astype(f32)
    target = jnp.concatenate(
        [one_hot(value_ranks[:, j * DL : j * DL + 1] == lane_rank) for j in range(groups)],
        axis=0,
    )
    result = dot(jnp.concatenate(split(terms), axis=0), target)
    grad[...] = grad_scale * (result[:DL] + result[DL:])

    arrivals.wait_send()
    for i, (_, _, step_x, step_y) in enumerate(faces):

        @pl.when(inside(step_x, step_y))
        def _():
            face_copy(i).wait_send()


def per_device(
    adjoint_e, adjoint_h, material, inv_eps, forward_design, cell_slot, tile_pillars, pillar_rank
):
    count_x, count_y = lax.axis_size("gx"), lax.axis_size("gy")
    devices = count_x * count_y
    _, cx, cy, nz = adjoint_e.shape
    slots = tile_pillars.shape[2]
    ranks = pillar_rank.reshape(-1, LANES)
    rank_rows = ranks.shape[0] // count_x
    owned = pillar_rank.shape[0] // devices
    anywhere = pl.BlockSpec(memory_space=pl.ANY)
    vmem = pl.BlockSpec(memory_space=pltpu.VMEM)
    return pl.pallas_call(
        functools.partial(kernel, count_x, count_y),
        out_shape=(
            jax.ShapeDtypeStruct(adjoint_e.shape, bf16),
            jax.ShapeDtypeStruct(adjoint_h.shape, bf16),
            jax.ShapeDtypeStruct((DL, owned), f32),
        ),
        in_specs=[
            anywhere,
            anywhere,
            anywhere,
            pl.BlockSpec(memory_space=pltpu.SMEM),
            anywhere,
            anywhere,
            anywhere,
            anywhere,
        ],
        out_specs=(vmem, vmem, vmem),
        scratch_shapes=[
            pltpu.VMEM((3, cx + 1, cy, nz), bf16),
            pltpu.VMEM((3, cx, cy, nz), bf16),
            pltpu.VMEM((cx, cy, nz), jnp.int32),
            pltpu.VMEM((3, cx, cy, nz), bf16),
            pltpu.VMEM((cx, cy), jnp.int32),
            pltpu.VMEM((count_y, slots), jnp.int32),
            pltpu.VMEM((rank_rows, LANES), jnp.int32),
            pltpu.VMEM((LANES, LANES), f32),
            pltpu.VMEM((slots, 2 * nz), f32),
            pltpu.VMEM((8, cx, nz), f32),
            pltpu.VMEM((2, cx, nz), bf16),
            pltpu.VMEM((5, cx, nz), bf16),
            pltpu.VMEM((2, cy, nz), bf16),
            pltpu.VMEM((3, cy, nz), bf16),
            pltpu.VMEM((2, cy, nz), bf16),
            pltpu.VMEM((2, cx, nz), bf16),
            pltpu.VMEM((5, cx, nz), bf16),
            pltpu.VMEM((16, nz), bf16),
            pltpu.VMEM((16, nz), bf16),
            pltpu.VMEM((2, cx, nz), f32),
            pltpu.VMEM((2, cx, nz), f32),
            pltpu.VMEM((devices * BLOCK, LANES), f32),
            pltpu.VMEM((devices * BLOCK, LANES), f32),
            pltpu.SemaphoreType.DMA((7,)),
            pltpu.SemaphoreType.DMA((7,)),
            pltpu.SemaphoreType.DMA((7,)),
            pltpu.SemaphoreType.DMA,
            pltpu.SemaphoreType.DMA,
        ],
        compiler_params=pltpu.CompilerParams(
            collective_id=0, has_side_effects=True, vmem_limit_bytes=48 * 1024 * 1024
        ),
    )(
        adjoint_e,
        adjoint_h,
        material,
        inv_eps,
        forward_design,
        cell_slot,
        tile_pillars,
        ranks,
    )


def solution(mesh):
    return jax.shard_map(
        per_device,
        mesh=mesh,
        in_specs=(
            P(None, "gx", "gy", None),
            P(None, "gx", "gy", None),
            P("gx", "gy", None),
            P(),
            P(None, "gx", "gy", None),
            P("gx", "gy"),
            P(),
            P(),
        ),
        out_specs=(P(None, "gx", "gy", None), P(None, "gx", "gy", None), P(None, ("gx", "gy"))),
        check_vma=False,
    )
```

time: 223 us -> 27.7 us (0.12)
  local copies, waits for them, and re-layouts: 113 us -> 8.59 us
  matrix products: 46 us -> 0 us
  starting transfers between devices: 23.5 us -> 0 us
  other arithmetic: 21 us -> 0 us
  Pallas kernels: 0 us -> 18.1 us
  between operations: 14.5 us -> 0.66 us
    gather x2 -> x0, local copies, waits for them, and re-layouts: 90.5 us -> none  [per_device(): pillar_rank[jnp.maximum(tile_pillars, 0)]]
    dot_general x33 -> x0, matrix products: 46 us -> none  [the longest x32 43.8 us: add_tile(): jnp.dot(tile_terms, selector, precision=lax.Precision.HIGHEST, preferred_...]
    ppermute x8 -> x0, starting transfers between devices: 23.5 us -> none  [shifted(): return lax.ppermute(block, axis, route)]
    pallas_call x0 -> x1, Pallas kernels: none -> 18.1 us  [per_device(): pl.pallas_call(functools.partial(kernel, count_x, count_y), out_shape=(ja...]
    slice x16 -> x0, local copies, waits for them, and re-layouts: 10.8 us -> none  [the longest x3 4.5 us: join_next(): rest = lax.slice_in_dim(field, 1, field.shape[axis], axis=axis)]
    another operation x4 -> x0, other arithmetic: 8.69 us -> none  [the longest x3 8.51 us: per_device(): new_e = jnp.stack([enew_x, enew_y, enew_z]).astype(jnp.bfloat16)]
    convert_element_type x6 -> x0, other arithmetic: 7.45 us -> none  [the longest x2 3 us: per_device(): magnetic_z = new_h[2].astype(jnp.float32)]
    reduce_sum x2 -> x0, other arithmetic: 4.55 us -> none  [the longest x1 2.58 us: per_device(): jnp.sum(slab * forward_design.astype(jnp.float32), axis=0)]
  transfers between devices with their start and end apart: 9 -> 0, of which waited for: 1 -> 0; matrix products, arithmetic and copies ran while one was open for 60% -> 0% of each run, Pallas kernels for 0% -> 0%
where the time goes in v1:
time: 27.7 us; the launch traced here: 27.4 us
  Pallas kernels  18.1 us (65%)
  local copies, waits for them, and re-layouts  8.59 us (31%)
  between operations  0.66 us (2%)
    pallas_call x1, Pallas kernels, per_device(): pl.pallas_call(functools.partial(kernel, count_x, count_y), out_shape=(ja...  18.1 us
    unnamed x15, local copies, waits for them, and re-layouts  8.59 us

profile of v1, /device:TPU:0, one launch (start us, length us, event | category | flops | bytes accessed | tf_op | source)
XLA Modules:
  0.0 27.4 jit_solution(8557325541719881698)
XLA Ops:
  0.6 0.0 copy-start
  0.6 1.4 %copy-done = bf16[3,32,64,128]{3,2,1,0:T(8,128)(2,1)S(1)} copy-done((bf16[3,32,64,128]{3,2,1,0:T(8,128)(2,1)S(1)}, bf16[3,32,64,128]{3,2,1,0:T(8,128)(2,1)}, u32[]{:S(2)}) %copy-start) | copy-done | bytes 1572888
  2.0 0.0 copy-start.1
  2.0 1.2 %copy-done.1 = s32[32,64,128]{2,1,0:T(8,128)S(1)} copy-done((s32[32,64,128]{2,1,0:T(8,128)S(1)}, s32[32,64,128]{2,1,0:T(8,128)}, u32[]{:S(2)}) %copy-start.1) | copy-done | bytes 1048600
  3.3 0.0 copy-start.2
  3.3 0.8 %copy-done.2 = s32[4,8,512]{2,1,0:T(8,128)S(1)} copy-done((s32[4,8,512]{2,1,0:T(8,128)S(1)}, s32[4,8,512]{2,1,0:T(8,128)}, u32[]{:S(2)}) %copy-start.2) | copy-done | bytes 65560
  4.1 0.0 copy-start.3
  4.1 0.8 %copy-done.3 = s32[16384]{0:T(1024)S(1)} copy-done((s32[16384]{0:T(1024)S(1)}, s32[16384]{0:T(1024)}, u32[]{:S(2)}) %copy-start.3) | copy-done | bytes 65560
  4.9 0.0 copy-start.4
  4.9 0.7 %copy-done.4 = s32[32,64]{1,0:T(8,128)S(1)} copy-done((s32[32,64]{1,0:T(8,128)S(1)}, s32[32,64]{1,0:T(8,128)}, u32[]{:S(2)}) %copy-start.4) | copy-done | bytes 8216
  5.7 0.0 copy-start.5
  5.7 0.7 %copy-done.5 = f32[4]{0:T(128)S(1)} copy-done((f32[4]{0:T(128)S(1)}, f32[4]{0:T(128)}, u32[]{:S(2)}) %copy-start.5) | copy-done | bytes 40
  6.3 18.1 %shard_map.103 = (bf16[3,32,64,128]{3,2,1,0:T(8,128)(2,1)S(1)}, bf16[3,32,64,128]{3,2,1,0:T(8,128)(2,1)S(1)}, f32[32,512]{1,0:T(8,128)S(1)}) custom-call(bf16[3,32,64,128]{3,2,1,0:T(8,128)(2,1)S(1)} %copy-done, bf16[3,32,64,128]{3,2,1,0:T(8,128)(2,1)} %h_hbm.1, s32[32,64,128]{2,1,0:T(8,128)S(1)} %copy-done.1, f32[4]{0:T(128)S(1)} %copy-done.5, ...), custom_call_target="tpu_custom_call" | custom-call | tf_op jit(solution)/shard_map/pallas_call | solution.py:420
  24.5 1.1 %copy.14 = bf16[3,32,64,128]{3,2,1,0:T(8,128)(2,1)} copy(bf16[3,32,64,128]{3,2,1,0:T(8,128)(2,1)S(1)} %get-tuple-element.6) | data formatting | bytes 3145728
  25.6 1.1 %copy.15 = bf16[3,32,64,128]{3,2,1,0:T(8,128)(2,1)} copy(bf16[3,32,64,128]{3,2,1,0:T(8,128)(2,1)S(1)} %get-tuple-element.7) | data formatting | bytes 3145728
  26.8 0.6 %copy.16 = f32[32,512]{1,0:T(8,128)} copy(f32[32,512]{1,0:T(8,128)S(1)} %get-tuple-element.8) | data formatting | bytes 131072
Async XLA Ops:
  0.6 1.4 %copy-start = (bf16[3,32,64,128]{3,2,1,0:T(8,128)(2,1)S(1)}, bf16[3,32,64,128]{3,2,1,0:T(8,128)(2,1)}, u32[]{:S(2)}) copy-start(bf16[3,32,64,128]{3,2,1,0:T(8,128)(2,1)} %e_hbm.1) | copy-start | bytes 4718596
  2.0 1.2 %copy-start.1 = (s32[32,64,128]{2,1,0:T(8,128)S(1)}, s32[32,64,128]{2,1,0:T(8,128)}, u32[]{:S(2)}) copy-start(s32[32,64,128]{2,1,0:T(8,128)} %m_hbm.1) | copy-start | bytes 3145732
  3.3 0.8 %copy-start.2 = (s32[4,8,512]{2,1,0:T(8,128)S(1)}, s32[4,8,512]{2,1,0:T(8,128)}, u32[]{:S(2)}) copy-start(s32[4,8,512]{2,1,0:T(8,128)} %tp_hbm.1) | copy-start | bytes 196612
  4.1 0.8 %copy-start.3 = (s32[16384]{0:T(1024)S(1)}, s32[16384]{0:T(1024)}, u32[]{:S(2)}) copy-start(s32[16384]{0:T(1024)} %param.15) | copy-start | bytes 196612
  4.9 0.7 %copy-start.4 = (s32[32,64]{1,0:T(8,128)S(1)}, s32[32,64]{1,0:T(8,128)}, u32[]{:S(2)}) copy-start(s32[32,64]{1,0:T(8,128)} %cs_hbm.1) | copy-start | bytes 24580
  5.7 0.7 %copy-start.5 = (f32[4]{0:T(128)S(1)}, f32[4]{0:T(128)}, u32[]{:S(2)}) copy-start(f32[4]{0:T(128)} %eps.1) | copy-start | bytes 52

commit v2 on v1

--- a/solution.py
+++ b/solution.py
@@ -36,24 +36,45 @@
     return high, (value - high.astype(f32)).astype(bf16)
 
 
-def kernel(
+def next_z(field):
+    size = field.shape[1]
+    return jnp.where(iota((1, size), 1) == size - 1, 0.0, pltpu.roll(field, size - 1, 1))
+
+
+def prior_z(field):
+    return jnp.where(iota((1, field.shape[1]), 1) == 0, 0.0, pltpu.roll(field, 1, 1))
+
+
+def next_row(field, edge):
+    size = field.shape[0]
+    return jnp.where(iota((size, 1), 0) == size - 1, edge, pltpu.roll(field, size - 1, 0))
+
+
+def prior_row(field, edge):
+    return jnp.where(iota((field.shape[0], 1), 0) == 0, edge, pltpu.roll(field, 1, 0))
+
+
+def exchange(
     count_x,
     count_y,
     e_hbm,
     h_hbm,
     m_hbm,
-    eps,
+    eps_hbm,
     f_hbm,
     cs_hbm,
     tp_hbm,
     pr_hbm,
-    ne,
+    e_v,
     nh,
-    grad,
-    e_v,
+    m_v,
+    factors,
+    hx_edge,
+    hy_edge,
+    recv,
     h_v,
-    m_v,
     f_v,
+    eps_v,
     cs_v,
     tp_v,
     pr_v,
@@ -70,9 +91,7 @@
     in_c1,
     in_c2,
     yn,
-    hy_edge,
     send,
-    recv,
     load_sem,
     face_send,
     face_recv,
@@ -97,12 +116,13 @@
         pltpu.make_async_copy(src, dst, load_sem.at[i])
         for i, (src, dst) in enumerate(
             [
+                (tp_hbm.at[gx], tp_v),
+                (pr_hbm.at[pl.ds(pl.multiple_of(gx * rank_rows, 8), rank_rows)], pr_v),
                 (e_hbm, e_v.at[:, pl.ds(0, cx)]),
                 (h_hbm, h_v),
-                (tp_hbm.at[gx], tp_v),
-                (pr_hbm.at[pl.ds(pl.multiple_of(gx * rank_rows, 8), rank_rows)], pr_v),
                 (cs_hbm, cs_v),
                 (f_hbm, f_v),
+                (eps_hbm, eps_v),
                 (m_hbm, m_v),
             ]
         )
@@ -124,66 +144,6 @@
 
     loads[0].wait()
     loads[1].wait()
-
-    def gather_rows(x, carry):
-        for c in range(3):
-            first = e_v[c, x, 0:16, :].astype(f32)
-            last = e_v[c, x, cy - 16 : cy, :].astype(f32)
-            stage[c, pl.ds(x, 1), :] = first[0:1]
-            stage[3 + c, pl.ds(x, 1), :] = last[15:16]
-        for k, c in enumerate((0, 2)):
-            stage[6 + k, pl.ds(x, 1), :] = h_v[c, x, cy - 16 : cy, :].astype(f32)[15:16]
-        return carry
-
-    lax.fori_loop(0, cx, gather_rows, 0)
-    out_y_prev[0] = stage[0].astype(bf16)
-    out_y_prev[1] = stage[2].astype(bf16)
-    for k in range(5):
-        out_y_next[k] = stage[3 + k].astype(bf16)
-
-    pl.semaphore_wait(barrier, devices - 1)
-
-    faces = [
-        (e_hbm.at[pl.ds(1, 2), 0], in_xn, -1, 0),
-        (out_y_prev, in_yn, 0, -1),
-        (e_hbm.at[:, cx - 1], in_xpe, 1, 0),
-        (h_hbm.at[pl.ds(1, 2), cx - 1], in_xph, 1, 0),
-        (out_y_next, in_yp, 0, 1),
-        (e_hbm.at[0, cx - 1, pl.ds(0, 16)], in_c1, 1, -1),
-        (e_hbm.at[1, 0, pl.ds(cy - 16, 16)], in_c2, -1, 1),
-    ]
-
-    def inside(step_x, step_y):
-        there = None
-        for at, step, count in ((gx, step_x, count_x), (gy, step_y, count_y)):
-            if step:
-                fits = at + step < count if step > 0 else at + step >= 0
-                there = fits if there is None else jnp.logical_and(there, fits)
-        return there
-
-    def face_copy(i):
-        source, landing, step_x, step_y = faces[i]
-        return pltpu.make_async_remote_copy(
-            src_ref=source,
-            dst_ref=landing,
-            send_sem=face_send.at[i],
-            recv_sem=face_recv.at[i],
-            device_id=(gx + step_x, gy + step_y),
-            device_id_type=MESH,
-        )
-
-    for i, (_, landing, step_x, step_y) in enumerate(faces):
-
-        @pl.when(inside(step_x, step_y))
-        def _():
-            face_copy(i).start()
-
-        @pl.when(jnp.logical_not(inside(-step_x, -step_y)))
-        def _():
-            landing[...] = jnp.zeros(landing.shape, landing.dtype)
-
-    loads[2].wait()
-    loads[3].wait()
     tile_row = iota(tp_v.shape, 0) == gy
     ids = jnp.sum(jnp.where(tile_row, tp_v[...], 0), axis=0, keepdims=True)
     listed = ids >= 0
@@ -226,6 +186,66 @@
             lane_group == j, rank_lines[j * LANES : (j + 1) * LANES], rank_block
         )
 
+    loads[2].wait()
+    loads[3].wait()
+
+    def gather_rows(x, carry):
+        for c in range(3):
+            first = e_v[c, x, 0:16, :].astype(f32)
+            last = e_v[c, x, cy - 16 : cy, :].astype(f32)
+            stage[c, pl.ds(x, 1), :] = first[0:1]
+            stage[3 + c, pl.ds(x, 1), :] = last[15:16]
+        for k, c in enumerate((0, 2)):
+            stage[6 + k, pl.ds(x, 1), :] = h_v[c, x, cy - 16 : cy, :].astype(f32)[15:16]
+        return carry
+
+    lax.fori_loop(0, cx, gather_rows, 0, unroll=4)
+    out_y_prev[0] = stage[0].astype(bf16)
+    out_y_prev[1] = stage[2].astype(bf16)
+    for k in range(5):
+        out_y_next[k] = stage[3 + k].astype(bf16)
+
+    pl.semaphore_wait(barrier, devices - 1)
+
+    faces = [
+        (e_hbm.at[pl.ds(1, 2), 0], in_xn, -1, 0),
+        (out_y_prev, in_yn, 0, -1),
+        (e_hbm.at[:, cx - 1], in_xpe, 1, 0),
+        (h_hbm.at[pl.ds(1, 2), cx - 1], in_xph, 1, 0),
+        (out_y_next, in_yp, 0, 1),
+        (e_hbm.at[0, cx - 1, pl.ds(0, 16)], in_c1, 1, -1),
+        (e_hbm.at[1, 0, pl.ds(cy - 16, 16)], in_c2, -1, 1),
+    ]
+
+    def inside(step_x, step_y):
+        there = None
+        for at, step, count in ((gx, step_x, count_x), (gy, step_y, count_y)):
+            if step:
+                fits = at + step < count if step > 0 else at + step >= 0
+                there = fits if there is None else jnp.logical_and(there, fits)
+        return there
+
+    def face_copy(i):
+        source, landing, step_x, step_y = faces[i]
+        return pltpu.make_async_remote_copy(
+            src_ref=source,
+            dst_ref=landing,
+            send_sem=face_send.at[i],
+            recv_sem=face_recv.at[i],
+            device_id=(gx + step_x, gy + step_y),
+            device_id_type=MESH,
+        )
+
+    for i, (_, landing, step_x, step_y) in enumerate(faces):
+
+        @pl.when(inside(step_x, step_y))
+        def _():
+            face_copy(i).start()
+
+        @pl.when(jnp.logical_not(inside(-step_x, -step_y)))
+        def _():
+            landing[...] = jnp.zeros(landing.shape, landing.dtype)
+
     loads[4].wait()
     loads[5].wait()
     batch = 256 // cy
@@ -245,7 +265,7 @@
         return carry
 
     acc[...] = jnp.zeros_like(acc)
-    lax.fori_loop(0, cx // batch, add_cells, 0)
+    lax.fori_loop(0, cx // batch, add_cells, 0, unroll=2)
     sums = acc[:, :nz] + acc[:, nz:]
     sorted_sums = dot(order, jnp.concatenate(split(sums), axis=1)).astype(bf16)
     packed = jnp.concatenate(
@@ -261,9 +281,10 @@
         ],
         axis=0,
     )
-    pool_row, pool_lane = iota((groups * nz, LANES), 0), iota((groups * nz, LANES), 1)
-    pool_to = lax.div(pool_row, nz) * DL + lax.div(lax.rem(pool_row, nz), nz // DL)
-    pooled = dot(packed, one_hot(pool_to == pool_lane))
+    layer = lax.div(iota((nz, LANES), 0), nz // DL)
+    lane = iota((nz, LANES), 1)
+    pool = jnp.concatenate([one_hot(layer + j * DL == lane) for j in range(groups)], axis=0)
+    pooled = dot(packed, pool)
     pooled = pooled[:LANES] + pooled[LANES:]
     if 2 * rows < BLOCK:
         send[...] = jnp.zeros_like(send)
@@ -300,24 +321,6 @@
     for k in range(2):
         yn[k] = in_yn[k].astype(f32)
 
-    last_lane = iota((1, nz), 1) == nz - 1
-    first_lane = iota((1, nz), 1) == 0
-
-    def next_z(field):
-        return jnp.where(last_lane, 0.0, pltpu.roll(field, nz - 1, 1))
-
-    def prior_z(field):
-        return jnp.where(first_lane, 0.0, pltpu.roll(field, 1, 1))
-
-    def next_row(field, edge):
-        size = field.shape[0]
-        return jnp.where(
-            iota((size, 1), 0) == size - 1, edge, pltpu.roll(field, size - 1, 0)
-        )
-
-    def prior_row(field, edge):
-        return jnp.where(iota((field.shape[0], 1), 0) == 0, edge, pltpu.roll(field, 1, 0))
-
     pe_x, pe_y, pe_z, ph_x, ph_z = [in_yp[k].astype(f32) for k in range(5)]
     first_x, first_z = stage[0], stage[2]
     edge_x = ph_x - courant * ((first_z - pe_z) - (next_z(pe_y) - pe_y))
@@ -334,40 +337,27 @@
     corner = in_c1[...].astype(f32)[0:1]
     back_z = ph_z - courant * ((first_y - pe_y) - (next_row(pe_x, corner) - pe_x))
     keep_x = gx > 0
-    back_y = jnp.where(keep_x, back_y, 0.0).astype(bf16)
-    back_z = jnp.where(keep_x, back_z, 0.0).astype(bf16)
-
-    loads[6].wait()
-    factors = [courant * eps[k] for k in range(eps.shape[0])]
-
-    def update(x, carry):
-        back_y, back_z = [value.astype(f32) for value in carry]
+    hx_edge[0] = jnp.where(keep_x, back_y, 0.0).astype(bf16)
+    hx_edge[1] = jnp.where(keep_x, back_z, 0.0).astype(bf16)
+
+    def update_h(x, carry):
         e_x, e_y, e_z = [e_v[c, x].astype(f32) for c in range(3)]
         nx_y, nx_z = [e_v[c, x + 1].astype(f32) for c in (1, 2)]
         ny_x, ny_z = [yn[k, pl.ds(x, 1), :] for k in range(2)]
         d_y_z, d_z_y = next_row(e_z, ny_z) - e_z, next_z(e_y) - e_y
-        h_x = (h_v[0, x].astype(f32) - courant * (d_y_z - d_z_y)).astype(bf16)
+        nh[0, x] = (h_v[0, x].astype(f32) - courant * (d_y_z - d_z_y)).astype(bf16)
         d_z_x, d_x_z = next_z(e_x) - e_x, nx_z - e_z
-        h_y = (h_v[1, x].astype(f32) - courant * (d_z_x - d_x_z)).astype(bf16)
+        nh[1, x] = (h_v[1, x].astype(f32) - courant * (d_z_x - d_x_z)).astype(bf16)
         d_x_y, d_y_x = nx_y - e_y, next_row(e_x, ny_x) - e_x
-        h_z = (h_v[2, x].astype(f32) - courant * (d_x_y - d_y_x)).astype(bf16)
-        nh[0, x], nh[1, x], nh[2, x] = h_x, h_y, h_z
-        ahead = (h_y, h_z)
-        h_x, h_y, h_z = h_x.astype(f32), h_y.astype(f32), h_z.astype(f32)
-        before_x, before_z = [hy_edge[k, pl.ds(x, 1), :] for k in range(2)]
-        material = m_v[x]
-        factor = jnp.full(material.shape, factors[-1], f32)
-        for which in range(len(factors) - 1):
-            factor = jnp.where(material == which, factors[which], factor)
-        b_y_z, b_z_y = h_z - prior_row(h_z, before_z), h_y - prior_z(h_y)
-        ne[0, x] = (e_x + factor * (b_y_z - b_z_y)).astype(bf16)
-        b_z_x, b_x_z = h_x - prior_z(h_x), h_z - back_z
-        ne[1, x] = (e_y + factor * (b_z_x - b_x_z)).astype(bf16)
-        b_x_y, b_y_x = h_y - back_y, h_x - prior_row(h_x, before_x)
-        ne[2, x] = (e_z + factor * (b_x_y - b_y_x)).astype(bf16)
-        return ahead
-
-    lax.fori_loop(0, cx, update, (back_y, back_z))
+        nh[2, x] = (h_v[2, x].astype(f32) - courant * (d_x_y - d_y_x)).astype(bf16)
+        return carry
+
+    lax.fori_loop(0, cx, update_h, 0, unroll=4)
+
+    loads[6].wait()
+    for k in range(eps_v.shape[0]):
+        factors[k : k + 1, :] = jnp.full((1, LANES), courant * eps_v[k], f32)
+    loads[7].wait()
 
     others = pl.ds(0, (devices - 1) * BLOCK)
     arrivals = pltpu.make_async_remote_copy(
@@ -379,6 +369,51 @@
         device_id_type=MESH,
     )
     arrivals.wait_recv()
+    arrivals.wait_send()
+    for i, (_, _, step_x, step_y) in enumerate(faces):
+
+        @pl.when(inside(step_x, step_y))
+        def _():
+            face_copy(i).wait_send()
+
+
+def finish(
+    materials,
+    e_v,
+    nh_v,
+    m_v,
+    factors,
+    hx_edge,
+    hy_edge,
+    recv,
+    ne,
+    nh,
+    grad,
+    ne_v,
+    grad_v,
+    store_sem,
+):
+    _, cx, cy, nz = nh_v.shape
+    devices = recv.shape[0] // BLOCK
+    owned = grad.shape[1]
+    groups = LANES // DL
+    rows = owned // devices // groups
+    chunks = 4
+    depth = cx // chunks
+
+    stores = [
+        pltpu.make_async_copy(nh_v, nh, store_sem.at[0]),
+        pltpu.make_async_copy(grad_v, grad, store_sem.at[1]),
+    ] + [
+        pltpu.make_async_copy(
+            ne_v.at[:, pl.ds(k * depth, depth)],
+            ne.at[:, pl.ds(k * depth, depth)],
+            store_sem.at[2 + k],
+        )
+        for k in range(chunks)
+    ]
+    stores[0].start()
+
     values = jnp.concatenate(
         [recv[pl.ds(i, devices, stride=BLOCK), :] for i in range(rows)], axis=0
     )
@@ -395,14 +430,36 @@
         axis=0,
     )
     result = dot(jnp.concatenate(split(terms), axis=0), target)
-    grad[...] = grad_scale * (result[:DL] + result[DL:])
-
-    arrivals.wait_send()
-    for i, (_, _, step_x, step_y) in enumerate(faces):
-
-        @pl.when(inside(step_x, step_y))
-        def _():
-            face_copy(i).wait_send()
+    grad_v[...] = grad_scale * (result[:DL] + result[DL:])
+
+    stores[1].start()
+
+    row_factors = [factors[k : k + 1, :] for k in range(materials)]
+
+    def update_e(x, carry):
+        back_y, back_z = [value.astype(f32) for value in carry]
+        ahead = nh_v[1, x], nh_v[2, x]
+        h_x = nh_v[0, x].astype(f32)
+        h_y, h_z = [value.astype(f32) for value in ahead]
+        before_x, before_z = [hy_edge[k, pl.ds(x, 1), :] for k in range(2)]
+        material = m_v[x]
+        factor = jnp.broadcast_to(row_factors[-1], material.shape)
+        for which in range(materials - 1):
+            factor = jnp.where(material == which, row_factors[which], factor)
+        b_y_z, b_z_y = h_z - prior_row(h_z, before_z), h_y - prior_z(h_y)
+        ne_v[0, x] = (e_v[0, x].astype(f32) + factor * (b_y_z - b_z_y)).astype(bf16)
+        b_z_x, b_x_z = h_x - prior_z(h_x), h_z - back_z
+        ne_v[1, x] = (e_v[1, x].astype(f32) + factor * (b_z_x - b_x_z)).astype(bf16)
+        b_x_y, b_y_x = h_y - back_y, h_x - prior_row(h_x, before_x)
+        ne_v[2, x] = (e_v[2, x].astype(f32) + factor * (b_x_y - b_y_x)).astype(bf16)
+        return ahead
+
+    carry = hx_edge[0], hx_edge[1]
+    for k in range(chunks):
+        carry = lax.fori_loop(k * depth, (k + 1) * depth, update_e, carry, unroll=4)
+        stores[2 + k].start()
+    for store in stores:
+        store.wait()
 
 
 def per_device(
@@ -417,29 +474,36 @@
     owned = pillar_rank.shape[0] // devices
     anywhere = pl.BlockSpec(memory_space=pl.ANY)
     vmem = pl.BlockSpec(memory_space=pltpu.VMEM)
-    return pl.pallas_call(
-        functools.partial(kernel, count_x, count_y),
+    operands = [
+        pltpu.with_memory_space_constraint(operand, pltpu.HBM)
+        for operand in (
+            adjoint_e,
+            adjoint_h,
+            material,
+            inv_eps,
+            forward_design,
+            cell_slot,
+            tile_pillars,
+            ranks,
+        )
+    ]
+    kept = pl.pallas_call(
+        functools.partial(exchange, count_x, count_y),
         out_shape=(
-            jax.ShapeDtypeStruct(adjoint_e.shape, bf16),
-            jax.ShapeDtypeStruct(adjoint_h.shape, bf16),
-            jax.ShapeDtypeStruct((DL, owned), f32),
-        ),
-        in_specs=[
-            anywhere,
-            anywhere,
-            anywhere,
-            pl.BlockSpec(memory_space=pltpu.SMEM),
-            anywhere,
-            anywhere,
-            anywhere,
-            anywhere,
-        ],
-        out_specs=(vmem, vmem, vmem),
-        scratch_shapes=[
             pltpu.VMEM((3, cx + 1, cy, nz), bf16),
             pltpu.VMEM((3, cx, cy, nz), bf16),
             pltpu.VMEM((cx, cy, nz), jnp.int32),
+            pltpu.VMEM((8, LANES), f32),
+            pltpu.VMEM((2, cy, nz), bf16),
+            pltpu.VMEM((2, cx, nz), f32),
+            pltpu.VMEM((devices * BLOCK, LANES), f32),
+        ),
+        in_specs=[anywhere] * 8,
+        out_specs=(vmem,) * 7,
+        scratch_shapes=[
             pltpu.VMEM((3, cx, cy, nz), bf16),
+            pltpu.VMEM((3, cx, cy, nz), bf16),
+            pltpu.SMEM(inv_eps.shape, f32),
             pltpu.VMEM((cx, cy), jnp.int32),
             pltpu.VMEM((count_y, slots), jnp.int32),
             pltpu.VMEM((rank_rows, LANES), jnp.int32),
@@ -456,28 +520,33 @@
             pltpu.VMEM((16, nz), bf16),
             pltpu.VMEM((16, nz), bf16),
             pltpu.VMEM((2, cx, nz), f32),
-            pltpu.VMEM((2, cx, nz), f32),
             pltpu.VMEM((devices * BLOCK, LANES), f32),
-            pltpu.VMEM((devices * BLOCK, LANES), f32),
-            pltpu.SemaphoreType.DMA((7,)),
+            pltpu.SemaphoreType.DMA((8,)),
             pltpu.SemaphoreType.DMA((7,)),
             pltpu.SemaphoreType.DMA((7,)),
             pltpu.SemaphoreType.DMA,
             pltpu.SemaphoreType.DMA,
         ],
         compiler_params=pltpu.CompilerParams(
-            collective_id=0, has_side_effects=True, vmem_limit_bytes=48 * 1024 * 1024
+            collective_id=0, has_side_effects=True, vmem_limit_bytes=24 * 1024 * 1024
         ),
-    )(
-        adjoint_e,
-        adjoint_h,
-        material,
-        inv_eps,
-        forward_design,
-        cell_slot,
-        tile_pillars,
-        ranks,
-    )
+    )(*operands)
+    return pl.pallas_call(
+        functools.partial(finish, inv_eps.shape[0]),
+        out_shape=(
+            pltpu.HBM(adjoint_e.shape, bf16),
+            pltpu.HBM(adjoint_h.shape, bf16),
+            pltpu.HBM((DL, owned), f32),
+        ),
+        in_specs=[vmem] * 7,
+        out_specs=(anywhere,) * 3,
+        scratch_shapes=[
+            pltpu.VMEM((3, cx, cy, nz), bf16),
+            pltpu.VMEM((DL, owned), f32),
+            pltpu.SemaphoreType.DMA((6,)),
+        ],
+        compiler_params=pltpu.CompilerParams(vmem_limit_bytes=16 * 1024 * 1024),
+    )(*[pltpu.with_memory_space_constraint(value, pltpu.VMEM) for value in kept])
 
 
 def solution(mesh):

time: 27.7 us -> 17.2 us (0.62)
  local copies, waits for them, and re-layouts: 8.59 us -> 0 us
  Pallas kernels: 18.1 us -> 16.3 us
    unnamed x15 -> x0, local copies, waits for them, and re-layouts: 8.59 us -> none
    pallas_call x1 -> x2, Pallas kernels: 18.1 us -> 16.3 us  [the longest x1 13.7 us: per_device(): pl.pallas_call(functools.partial(exchange, count_x, count_y), out_shape=(...]
where the time goes in v2:
time: 17.2 us; the launch traced here: 16.9 us
  Pallas kernels  16.3 us (95%)
  between operations  0.64 us (4%)
    pallas_call x1, Pallas kernels, per_device(): pl.pallas_call(functools.partial(exchange, count_x, count_y), out_shape=(...  13.7 us
    pallas_call x1, Pallas kernels, per_device(): pl.pallas_call(functools.partial(finish, inv_eps.shape[0]), out_shape=(pl...  2.59 us

profile of v2, /device:TPU:0, one launch (start us, length us, event | category | flops | bytes accessed | tf_op | source)
XLA Modules:
  0.0 16.9 jit_solution(5150454170643967395)
XLA Ops:
  0.6 13.7 %shard_map.103 = (bf16[3,33,64,128]{3,2,1,0:T(8,128)(2,1)S(1)}, bf16[3,32,64,128]{3,2,1,0:T(8,128)(2,1)S(1)}, s32[32,64,128]{2,1,0:T(8,128)S(1)}, f32[8,128]{1,0...) custom-call(bf16[3,32,64,128]{3,2,1,0:T(8,128)(2,1)} %e_hbm.1, ...), custom_call_target="tpu_custom_call" | custom-call | tf_op jit(solution)/shard_map/pallas_call | solution.py:490
  14.3 2.6 %shard_map.104 = (bf16[3,32,64,128]{3,2,1,0:T(8,128)(2,1)}, bf16[3,32,64,128]{3,2,1,0:T(8,128)(2,1)}, f32[32,512]{1,0:T(8,128)}) custom-call(bf16[3,33,64,128]{3,2,1,0:T(8,128)(2,1)S(1)} %get-tuple-element.10.e_v, bf16[3,32,64,128]{3,2,1,0:T(8,128)(2,1)S(1)} %get-tuple-element.11.nh_v, s32[32,64,128]{2,1,0:T(8,128)S(1)} %get-tuple-element.12.m_v, ...), custom_call_target="tpu_custom_call" | custom-call | tf_op jit(solution)/shard_map/pallas_call | solution.py:534

commit v3 on v2

--- a/solution.py
+++ b/solution.py
@@ -29,6 +29,14 @@
 
 def one_hot(mask):
     return jnp.where(mask, 1.0, 0.0).astype(bf16)
+
+
+def hot_rows(count, row):
+    size = row.shape[1]
+    number = iota((count, size), 0).astype(jnp.int16).reshape(count // 16, 16, size)
+    entry = jnp.broadcast_to(row, (16, size)).astype(jnp.int16)
+    hot = jnp.where(number == entry[None], jnp.ones((), bf16), jnp.zeros((), bf16))
+    return hot.reshape(count, size)
 
 
 def split(value):
@@ -65,13 +73,13 @@
     cs_hbm,
     tp_hbm,
     pr_hbm,
+    ne,
+    nh,
+    recv,
     e_v,
-    nh,
     m_v,
-    factors,
     hx_edge,
     hy_edge,
-    recv,
     h_v,
     f_v,
     eps_v,
@@ -175,10 +183,18 @@
     owner, nth = lax.div(place, per_device), lax.rem(place, per_device)
     line = lax.div(nth, rows) * LANES + lax.rem(nth, rows) * devices + owner
     line = jnp.where(listed, line, -1)
-    chosen = iota((slots, slots), 0) == line
-    order = one_hot(chosen)
-    own_rank = lax.rem(slot_rank.astype(jnp.int32), owned).astype(f32)
-    rank_lines = jnp.sum(jnp.where(chosen, own_rank, 0.0), axis=1, keepdims=True)
+    order = hot_rows(slots, line)
+    own_rank = lax.rem(slot_rank.astype(jnp.int32), owned)
+    own_high = lax.shift_right_logical(own_rank, 8).astype(f32)
+    own_low = lax.bitwise_and(own_rank, 255).astype(f32)
+    rank_table = jnp.concatenate(
+        [jnp.broadcast_to(own, (LANES, slots)).astype(bf16) for own in (own_high, own_low)],
+        axis=0,
+    )
+    rank_lines = lax.dot_general(
+        order, rank_table, (((1,), (1,)), ((), ())), preferred_element_type=f32
+    )
+    rank_lines = 256.0 * rank_lines[:, :LANES] + rank_lines[:, LANES:]
     lane_group = lax.div(iota((LANES, LANES), 1), DL)
     rank_block = jnp.zeros((LANES, LANES), f32)
     for j in range(groups):
@@ -187,6 +203,26 @@
         )
 
     loads[2].wait()
+    loads[4].wait()
+    loads[5].wait()
+    batch = 256 // cy
+
+    def add_cells(g, carry):
+        slot_parts, parts = [], []
+        for a in range(batch):
+            x = g * batch + a
+            slot_parts.append(cs_v[pl.ds(x, 1), :])
+            density = e_v[0, x].astype(f32) * f_v[0, x].astype(f32)
+            for c in (1, 2):
+                density = density + e_v[c, x].astype(f32) * f_v[c, x].astype(f32)
+            parts.append(jnp.concatenate(split(density), axis=1))
+        cell_slots = jnp.concatenate(slot_parts, axis=1)
+        hot = hot_rows(slots, cell_slots)
+        acc[...] += dot(hot, jnp.concatenate(parts, axis=0))
+        return carry
+
+    acc[...] = jnp.zeros_like(acc)
+    lax.fori_loop(0, cx // batch, add_cells, 0, unroll=2)
     loads[3].wait()
 
     def gather_rows(x, carry):
@@ -246,26 +282,6 @@
         def _():
             landing[...] = jnp.zeros(landing.shape, landing.dtype)
 
-    loads[4].wait()
-    loads[5].wait()
-    batch = 256 // cy
-
-    def add_cells(g, carry):
-        slot_parts, parts = [], []
-        for a in range(batch):
-            x = g * batch + a
-            slot_parts.append(cs_v[pl.ds(x, 1), :])
-            density = e_v[0, x].astype(f32) * f_v[0, x].astype(f32)
-            for c in (1, 2):
-                density = density + e_v[c, x].astype(f32) * f_v[c, x].astype(f32)
-            parts.append(jnp.concatenate(split(density), axis=1))
-        cell_slots = jnp.concatenate(slot_parts, axis=1)
-        hot = one_hot(iota((slots, batch * cy), 0) == cell_slots)
-        acc[...] += dot(hot, jnp.concatenate(parts, axis=0))
-        return carry
-
-    acc[...] = jnp.zeros_like(acc)
-    lax.fori_loop(0, cx // batch, add_cells, 0, unroll=2)
     sums = acc[:, :nz] + acc[:, nz:]
     sorted_sums = dot(order, jnp.concatenate(split(sums), axis=1)).astype(bf16)
     packed = jnp.concatenate(
@@ -355,9 +371,29 @@
     lax.fori_loop(0, cx, update_h, 0, unroll=4)
 
     loads[6].wait()
-    for k in range(eps_v.shape[0]):
-        factors[k : k + 1, :] = jnp.full((1, LANES), courant * eps_v[k], f32)
     loads[7].wait()
+    materials = eps_v.shape[0]
+    factors = [courant * eps_v[k] for k in range(materials)]
+
+    def update_e(x, carry):
+        back_y, back_z = [value.astype(f32) for value in carry]
+        ahead = nh[1, x], nh[2, x]
+        h_x = nh[0, x].astype(f32)
+        h_y, h_z = [value.astype(f32) for value in ahead]
+        before_x, before_z = [hy_edge[k, pl.ds(x, 1), :] for k in range(2)]
+        material = m_v[x]
+        factor = jnp.full(material.shape, factors[-1], f32)
+        for which in range(materials - 1):
+            factor = jnp.where(material == which, factors[which], factor)
+        b_y_z, b_z_y = h_z - prior_row(h_z, before_z), h_y - prior_z(h_y)
+        ne[0, x] = (e_v[0, x].astype(f32) + factor * (b_y_z - b_z_y)).astype(bf16)
+        b_z_x, b_x_z = h_x - prior_z(h_x), h_z - back_z
+        ne[1, x] = (e_v[1, x].astype(f32) + factor * (b_z_x - b_x_z)).astype(bf16)
+        b_x_y, b_y_x = h_y - back_y, h_x - prior_row(h_x, before_x)
+        ne[2, x] = (e_v[2, x].astype(f32) + factor * (b_x_y - b_y_x)).astype(bf16)
+        return ahead
+
+    lax.fori_loop(0, cx, update_e, (hx_edge[0], hx_edge[1]), unroll=4)
 
     others = pl.ds(0, (devices - 1) * BLOCK)
     arrivals = pltpu.make_async_remote_copy(
@@ -378,41 +414,26 @@
 
 
 def finish(
-    materials,
-    e_v,
+    ne_v,
     nh_v,
-    m_v,
-    factors,
-    hx_edge,
-    hy_edge,
     recv,
     ne,
     nh,
     grad,
-    ne_v,
     grad_v,
     store_sem,
 ):
-    _, cx, cy, nz = nh_v.shape
     devices = recv.shape[0] // BLOCK
     owned = grad.shape[1]
     groups = LANES // DL
     rows = owned // devices // groups
-    chunks = 4
-    depth = cx // chunks
 
     stores = [
-        pltpu.make_async_copy(nh_v, nh, store_sem.at[0]),
-        pltpu.make_async_copy(grad_v, grad, store_sem.at[1]),
-    ] + [
-        pltpu.make_async_copy(
-            ne_v.at[:, pl.ds(k * depth, depth)],
-            ne.at[:, pl.ds(k * depth, depth)],
-            store_sem.at[2 + k],
-        )
-        for k in range(chunks)
+        pltpu.make_async_copy(src, dst, store_sem.at[i])
+        for i, (src, dst) in enumerate([(ne_v, ne), (nh_v, nh), (grad_v, grad)])
     ]
     stores[0].start()
+    stores[1].start()
 
     values = jnp.concatenate(
         [recv[pl.ds(i, devices, stride=BLOCK), :] for i in range(rows)], axis=0
@@ -432,32 +453,7 @@
     result = dot(jnp.concatenate(split(terms), axis=0), target)
     grad_v[...] = grad_scale * (result[:DL] + result[DL:])
 
-    stores[1].start()
-
-    row_factors = [factors[k : k + 1, :] for k in range(materials)]
-
-    def update_e(x, carry):
-        back_y, back_z = [value.astype(f32) for value in carry]
-        ahead = nh_v[1, x], nh_v[2, x]
-        h_x = nh_v[0, x].astype(f32)
-        h_y, h_z = [value.astype(f32) for value in ahead]
-        before_x, before_z = [hy_edge[k, pl.ds(x, 1), :] for k in range(2)]
-        material = m_v[x]
-        factor = jnp.broadcast_to(row_factors[-1], material.shape)
-        for which in range(materials - 1):
-            factor = jnp.where(material == which, row_factors[which], factor)
-        b_y_z, b_z_y = h_z - prior_row(h_z, before_z), h_y - prior_z(h_y)
-        ne_v[0, x] = (e_v[0, x].astype(f32) + factor * (b_y_z - b_z_y)).astype(bf16)
-        b_z_x, b_x_z = h_x - prior_z(h_x), h_z - back_z
-        ne_v[1, x] = (e_v[1, x].astype(f32) + factor * (b_z_x - b_x_z)).astype(bf16)
-        b_x_y, b_y_x = h_y - back_y, h_x - prior_row(h_x, before_x)
-        ne_v[2, x] = (e_v[2, x].astype(f32) + factor * (b_x_y - b_y_x)).astype(bf16)
-        return ahead
-
-    carry = hx_edge[0], hx_edge[1]
-    for k in range(chunks):
-        carry = lax.fori_loop(k * depth, (k + 1) * depth, update_e, carry, unroll=4)
-        stores[2 + k].start()
+    stores[2].start()
     for store in stores:
         store.wait()
 
@@ -490,17 +486,17 @@
     kept = pl.pallas_call(
         functools.partial(exchange, count_x, count_y),
         out_shape=(
-            pltpu.VMEM((3, cx + 1, cy, nz), bf16),
             pltpu.VMEM((3, cx, cy, nz), bf16),
-            pltpu.VMEM((cx, cy, nz), jnp.int32),
-            pltpu.VMEM((8, LANES), f32),
-            pltpu.VMEM((2, cy, nz), bf16),
-            pltpu.VMEM((2, cx, nz), f32),
+            pltpu.VMEM((3, cx, cy, nz), bf16),
             pltpu.VMEM((devices * BLOCK, LANES), f32),
         ),
         in_specs=[anywhere] * 8,
-        out_specs=(vmem,) * 7,
+        out_specs=(vmem,) * 3,
         scratch_shapes=[
+            pltpu.VMEM((3, cx + 1, cy, nz), bf16),
+            pltpu.VMEM((cx, cy, nz), jnp.int32),
+            pltpu.VMEM((2, cy, nz), bf16),
+            pltpu.VMEM((2, cx, nz), f32),
             pltpu.VMEM((3, cx, cy, nz), bf16),
             pltpu.VMEM((3, cx, cy, nz), bf16),
             pltpu.SMEM(inv_eps.shape, f32),
@@ -532,18 +528,17 @@
         ),
     )(*operands)
     return pl.pallas_call(
-        functools.partial(finish, inv_eps.shape[0]),
+        finish,
         out_shape=(
             pltpu.HBM(adjoint_e.shape, bf16),
             pltpu.HBM(adjoint_h.shape, bf16),
             pltpu.HBM((DL, owned), f32),
         ),
-        in_specs=[vmem] * 7,
+        in_specs=[vmem] * 3,
         out_specs=(anywhere,) * 3,
         scratch_shapes=[
-            pltpu.VMEM((3, cx, cy, nz), bf16),
             pltpu.VMEM((DL, owned), f32),
-            pltpu.SemaphoreType.DMA((6,)),
+            pltpu.SemaphoreType.DMA((3,)),
         ],
         compiler_params=pltpu.CompilerParams(vmem_limit_bytes=16 * 1024 * 1024),
     )(*[pltpu.with_memory_space_constraint(value, pltpu.VMEM) for value in kept])

time: 17.2 us -> 17.9 us (1.041)
  the two profiles are of different devices: /device:TPU:0 before, /device:TPU:1 now
where the time goes in v3:
time: 17.9 us; the launch traced here: 17.7 us
  Pallas kernels  17.1 us (96%)
  between operations  0.64 us (4%)
    pallas_call x1, Pallas kernels, per_device(): pl.pallas_call(functools.partial(exchange, count_x, count_y), out_shape=(...  15.3 us
    pallas_call x1, Pallas kernels, per_device(): pl.pallas_call(finish, out_shape=(pltpu.HBM(adjoint_e.shape, bf16), pltpu...  1.71 us

profile of v3, /device:TPU:1, one launch (start us, length us, event | category | flops | bytes accessed | tf_op | source)
XLA Modules:
  0.0 17.7 jit_solution(7484666976419268144)
XLA Ops:
  0.6 15.3 %shard_map.103 = (bf16[3,32,64,128]{3,2,1,0:T(8,128)(2,1)S(1)}, bf16[3,32,64,128]{3,2,1,0:T(8,128)(2,1)S(1)}, f32[256,128]{1,0:T(8,128)S(1)}) custom-call(bf16[3,32,64,128]{3,2,1,0:T(8,128)(2,1)} %e_hbm.1, bf16[3,32,64,128]{3,2,1,0:T(8,128)(2,1)} %h_hbm.1, s32[32,64,128]{2,1,0:T(8,128)} %m_hbm.1, f32[4]{0:T(128)} %eps_hbm.1, bf16[3,32,64,128]{3,2,1,0:T(8,128)(2,1)} %f_hbm.1, ...), custom_call_target="tpu_custom_call" | custom-call | tf_op jit(solution)/shard_map/pallas_call | solution.py:486
  16.0 1.7 %shard_map.104 = (bf16[3,32,64,128]{3,2,1,0:T(8,128)(2,1)}, bf16[3,32,64,128]{3,2,1,0:T(8,128)(2,1)}, f32[32,512]{1,0:T(8,128)}) custom-call(bf16[3,32,64,128]{3,2,1,0:T(8,128)(2,1)S(1)} %get-tuple-element.6.ne_v, bf16[3,32,64,128]{3,2,1,0:T(8,128)(2,1)S(1)} %get-tuple-element.7.nh_v, f32[256,128]{1,0:T(8,128)S(1)} %get-tuple-element.8.recv), custom_call_target="tpu_custom_call" | custom-call | tf_op jit(solution)/shard_map/pallas_call | solution.py:530

commit v4 on v3

--- a/solution.py
+++ b/solution.py
@@ -78,7 +78,6 @@
     recv,
     e_v,
     m_v,
-    hx_edge,
     hy_edge,
     h_v,
     f_v,
@@ -244,13 +243,13 @@
     pl.semaphore_wait(barrier, devices - 1)
 
     faces = [
+        (out_y_prev, in_yn, 0, -1),
+        (out_y_next, in_yp, 0, 1),
+        (e_hbm.at[1, 0, pl.ds(cy - 16, 16)], in_c2, -1, 1),
         (e_hbm.at[pl.ds(1, 2), 0], in_xn, -1, 0),
-        (out_y_prev, in_yn, 0, -1),
         (e_hbm.at[:, cx - 1], in_xpe, 1, 0),
         (h_hbm.at[pl.ds(1, 2), cx - 1], in_xph, 1, 0),
-        (out_y_next, in_yp, 0, 1),
         (e_hbm.at[0, cx - 1, pl.ds(0, 16)], in_c1, 1, -1),
-        (e_hbm.at[1, 0, pl.ds(cy - 16, 16)], in_c2, -1, 1),
     ]
 
     def inside(step_x, step_y):
@@ -326,35 +325,16 @@
     lax.fori_loop(1, devices, send_part, 0)
     recv[mine, :] = send[mine, :]
 
-    for i, (_, _, step_x, step_y) in enumerate(faces):
-
-        @pl.when(inside(-step_x, -step_y))
-        def _():
-            face_copy(i).wait_recv()
-
-    for c in (1, 2):
-        e_v[c, cx] = in_xn[c - 1]
+    def await_faces(which):
+        for i in which:
+
+            @pl.when(inside(-faces[i][2], -faces[i][3]))
+            def _():
+                face_copy(i).wait_recv()
+
+    await_faces([0])
     for k in range(2):
         yn[k] = in_yn[k].astype(f32)
-
-    pe_x, pe_y, pe_z, ph_x, ph_z = [in_yp[k].astype(f32) for k in range(5)]
-    first_x, first_z = stage[0], stage[2]
-    edge_x = ph_x - courant * ((first_z - pe_z) - (next_z(pe_y) - pe_y))
-    corner = in_c2[...].astype(f32)[15:16]
-    edge_z = ph_z - courant * ((next_row(pe_y, corner) - pe_y) - (first_x - pe_x))
-    keep_y = gy > 0
-    hy_edge[0] = jnp.where(keep_y, edge_x, 0.0).astype(bf16).astype(f32)
-    hy_edge[1] = jnp.where(keep_y, edge_z, 0.0).astype(bf16).astype(f32)
-
-    pe_x, pe_y, pe_z = [in_xpe[k].astype(f32) for k in range(3)]
-    ph_y, ph_z = [in_xph[k].astype(f32) for k in range(2)]
-    first_y, first_z = e_v[1, 0].astype(f32), e_v[2, 0].astype(f32)
-    back_y = ph_y - courant * ((next_z(pe_x) - pe_x) - (first_z - pe_z))
-    corner = in_c1[...].astype(f32)[0:1]
-    back_z = ph_z - courant * ((first_y - pe_y) - (next_row(pe_x, corner) - pe_x))
-    keep_x = gx > 0
-    hx_edge[0] = jnp.where(keep_x, back_y, 0.0).astype(bf16)
-    hx_edge[1] = jnp.where(keep_x, back_z, 0.0).astype(bf16)
 
     def update_h(x, carry):
         e_x, e_y, e_z = [e_v[c, x].astype(f32) for c in range(3)]
@@ -368,7 +348,25 @@
         nh[2, x] = (h_v[2, x].astype(f32) - courant * (d_x_y - d_y_x)).astype(bf16)
         return carry
 
-    lax.fori_loop(0, cx, update_h, 0, unroll=4)
+    unrolled = 4
+    main = (cx - 1) // unrolled * unrolled
+    lax.fori_loop(0, main, update_h, 0, unroll=unrolled)
+    for x in range(main, cx - 1):
+        update_h(x, 0)
+    await_faces([3])
+    for c in (1, 2):
+        e_v[c, cx] = in_xn[c - 1]
+    update_h(cx - 1, 0)
+
+    await_faces([1, 2])
+    pe_x, pe_y, pe_z, ph_x, ph_z = [in_yp[k].astype(f32) for k in range(5)]
+    first_x, first_z = stage[0], stage[2]
+    edge_x = ph_x - courant * ((first_z - pe_z) - (next_z(pe_y) - pe_y))
+    corner = in_c2[...].astype(f32)[15:16]
+    edge_z = ph_z - courant * ((next_row(pe_y, corner) - pe_y) - (first_x - pe_x))
+    keep_y = gy > 0
+    hy_edge[0] = jnp.where(keep_y, edge_x, 0.0).astype(bf16).astype(f32)
+    hy_edge[1] = jnp.where(keep_y, edge_z, 0.0).astype(bf16).astype(f32)
 
     loads[6].wait()
     loads[7].wait()
@@ -393,7 +391,23 @@
         ne[2, x] = (e_v[2, x].astype(f32) + factor * (b_x_y - b_y_x)).astype(bf16)
         return ahead
 
-    lax.fori_loop(0, cx, update_e, (hx_edge[0], hx_edge[1]), unroll=4)
+    carry = nh[1, 0], nh[2, 0]
+    carry = lax.fori_loop(1, 1 + main, update_e, carry, unroll=unrolled)
+    for x in range(1 + main, cx):
+        carry = update_e(x, carry)
+
+    await_faces([4, 5, 6])
+    pe_x, pe_y, pe_z = [in_xpe[k].astype(f32) for k in range(3)]
+    ph_y, ph_z = [in_xph[k].astype(f32) for k in range(2)]
+    first_y, first_z = e_v[1, 0].astype(f32), e_v[2, 0].astype(f32)
+    back_y = ph_y - courant * ((next_z(pe_x) - pe_x) - (first_z - pe_z))
+    corner = in_c1[...].astype(f32)[0:1]
+    back_z = ph_z - courant * ((first_y - pe_y) - (next_row(pe_x, corner) - pe_x))
+    keep_x = gx > 0
+    edge_y = jnp.where(keep_x, back_y, 0.0).astype(bf16)
+    edge_z = jnp.where(keep_x, back_z, 0.0).astype(bf16)
+
+    update_e(0, (edge_y, edge_z))
 
     others = pl.ds(0, (devices - 1) * BLOCK)
     arrivals = pltpu.make_async_remote_copy(
@@ -495,7 +509,6 @@
         scratch_shapes=[
             pltpu.VMEM((3, cx + 1, cy, nz), bf16),
             pltpu.VMEM((cx, cy, nz), jnp.int32),
-            pltpu.VMEM((2, cy, nz), bf16),
             pltpu.VMEM((2, cx, nz), f32),
             pltpu.VMEM((3, cx, cy, nz), bf16),
             pltpu.VMEM((3, cx, cy, nz), bf16),

time: 17.9 us -> 16.1 us (0.90)
  the two profiles are of different devices: /device:TPU:1 before, /device:TPU:0 now
where the time goes in v4:
time: 16.1 us; the launch traced here: 15.9 us
  Pallas kernels  15.3 us (95%)
  between operations  0.64 us (4%)
    pallas_call x1, Pallas kernels, per_device(): pl.pallas_call(functools.partial(exchange, count_x, count_y), out_shape=(...  13.5 us
    pallas_call x1, Pallas kernels, per_device(): pl.pallas_call(finish, out_shape=(pltpu.HBM(adjoint_e.shape, bf16), pltpu...  1.71 us

profile of v4, /device:TPU:0, one launch (start us, length us, event | category | flops | bytes accessed | tf_op | source)
XLA Modules:
  0.0 15.9 jit_solution(800514291761456182)
XLA Ops:
  0.6 13.5 %shard_map.103 = (bf16[3,32,64,128]{3,2,1,0:T(8,128)(2,1)S(1)}, bf16[3,32,64,128]{3,2,1,0:T(8,128)(2,1)S(1)}, f32[256,128]{1,0:T(8,128)S(1)}) custom-call(bf16[3,32,64,128]{3,2,1,0:T(8,128)(2,1)} %e_hbm.1, bf16[3,32,64,128]{3,2,1,0:T(8,128)(2,1)} %h_hbm.1, s32[32,64,128]{2,1,0:T(8,128)} %m_hbm.1, f32[4]{0:T(128)} %eps_hbm.1, bf16[3,32,64,128]{3,2,1,0:T(8,128)(2,1)} %f_hbm.1, ...), custom_call_target="tpu_custom_call" | custom-call | tf_op jit(solution)/shard_map/pallas_call | solution.py:500
  14.2 1.7 %shard_map.104 = (bf16[3,32,64,128]{3,2,1,0:T(8,128)(2,1)}, bf16[3,32,64,128]{3,2,1,0:T(8,128)(2,1)}, f32[32,512]{1,0:T(8,128)}) custom-call(bf16[3,32,64,128]{3,2,1,0:T(8,128)(2,1)S(1)} %get-tuple-element.6.ne_v, bf16[3,32,64,128]{3,2,1,0:T(8,128)(2,1)S(1)} %get-tuple-element.7.nh_v, f32[256,128]{1,0:T(8,128)S(1)} %get-tuple-element.8.recv), custom_call_target="tpu_custom_call" | custom-call | tf_op jit(solution)/shard_map/pallas_call | solution.py:543

commit v5 on v4

--- a/solution.py
+++ b/solution.py
@@ -143,11 +143,17 @@
         device = lax.rem(me + step, devices)
         return device, (lax.div(device, count_y), lax.rem(device, count_y))
 
+    def each_partner(act):
+        main = (devices - 1) // 4 * 4
+        lax.fori_loop(1, 1 + main, act, 0, unroll=4)
+        for step in range(1 + main, devices):
+            act(step, 0)
+
     def greet(step, carry):
         pl.semaphore_signal(barrier, inc=1, device_id=partner(step)[1], device_id_type=MESH)
         return carry
 
-    lax.fori_loop(1, devices, greet, 0)
+    each_partner(greet)
 
     loads[0].wait()
     loads[1].wait()
@@ -194,12 +200,11 @@
         order, rank_table, (((1,), (1,)), ((), ())), preferred_element_type=f32
     )
     rank_lines = 256.0 * rank_lines[:, :LANES] + rank_lines[:, LANES:]
-    lane_group = lax.div(iota((LANES, LANES), 1), DL)
-    rank_block = jnp.zeros((LANES, LANES), f32)
-    for j in range(groups):
-        rank_block = jnp.where(
-            lane_group == j, rank_lines[j * LANES : (j + 1) * LANES], rank_block
-        )
+    lane = iota((devices, LANES), 1)
+    rank_block = jnp.zeros((devices, LANES), f32)
+    for k in range(per_device):
+        part = rank_lines[k * devices : (k + 1) * devices]
+        rank_block = jnp.where(lane == k, part, rank_block)
 
     loads[2].wait()
     loads[4].wait()
@@ -221,7 +226,7 @@
         return carry
 
     acc[...] = jnp.zeros_like(acc)
-    lax.fori_loop(0, cx // batch, add_cells, 0, unroll=2)
+    lax.fori_loop(0, cx // batch, add_cells, 0, unroll=4)
     loads[3].wait()
 
     def gather_rows(x, carry):
@@ -301,19 +306,18 @@
     pool = jnp.concatenate([one_hot(layer + j * DL == lane) for j in range(groups)], axis=0)
     pooled = dot(packed, pool)
     pooled = pooled[:LANES] + pooled[LANES:]
-    if 2 * rows < BLOCK:
-        send[...] = jnp.zeros_like(send)
     for i in range(rows):
         part = slice(i * devices, (i + 1) * devices)
         send[pl.ds(i, devices, stride=BLOCK), :] = pooled[part]
-        send[pl.ds(rows + i, devices, stride=BLOCK), :] = rank_block[part]
-
-    mine = pl.ds(pl.multiple_of(me * BLOCK, BLOCK), BLOCK)
+    send[pl.ds(rows, devices, stride=BLOCK), :] = rank_block
+
+    used = rows + 1
+    mine = pl.ds(pl.multiple_of(me * BLOCK, BLOCK), used)
 
     def send_part(step, carry):
         device, where = partner(step)
         pltpu.make_async_remote_copy(
-            src_ref=send.at[pl.ds(pl.multiple_of(device * BLOCK, BLOCK), BLOCK)],
+            src_ref=send.at[pl.ds(pl.multiple_of(device * BLOCK, BLOCK), used)],
             dst_ref=recv.at[mine],
             send_sem=part_send,
             recv_sem=part_recv,
@@ -322,7 +326,7 @@
         ).start()
         return carry
 
-    lax.fori_loop(1, devices, send_part, 0)
+    each_partner(send_part)
     recv[mine, :] = send[mine, :]
 
     def await_faces(which):
@@ -409,7 +413,7 @@
 
     update_e(0, (edge_y, edge_z))
 
-    others = pl.ds(0, (devices - 1) * BLOCK)
+    others = pl.ds(0, (devices - 1) * used)
     arrivals = pltpu.make_async_remote_copy(
         src_ref=send.at[others],
         dst_ref=recv.at[others],
@@ -452,16 +456,14 @@
     values = jnp.concatenate(
         [recv[pl.ds(i, devices, stride=BLOCK), :] for i in range(rows)], axis=0
     )
-    value_ranks = jnp.concatenate(
-        [recv[pl.ds(rows + i, devices, stride=BLOCK), :] for i in range(rows)], axis=0
-    )
+    value_ranks = recv[pl.ds(rows, devices, stride=BLOCK), :]
     turned_values = values.T
     terms = jnp.concatenate(
         [turned_values[j * DL : (j + 1) * DL] for j in range(groups)], axis=1
     )
-    lane_rank = iota((LANES, owned), 1).astype(f32)
+    lane_rank = iota((devices, owned), 1).astype(f32)
     target = jnp.concatenate(
-        [one_hot(value_ranks[:, j * DL : j * DL + 1] == lane_rank) for j in range(groups)],
+        [one_hot(value_ranks[:, k : k + 1] == lane_rank) for k in range(groups * rows)],
         axis=0,
     )
     result = dot(jnp.concatenate(split(terms), axis=0), target)

time: 16.1 us -> 15.6 us (0.969)
  Pallas kernels: 15.3 us -> 14.7 us
    pallas_call x1, Pallas kernels: 13.5 us -> 13 us  [per_device(): pl.pallas_call(functools.partial(exchange, count_x, count_y), out_shape=(...]
where the time goes in v5:
time: 15.6 us; the launch traced here: 15.4 us
  Pallas kernels  14.7 us (94%)
  between operations  0.64 us (4%)
    pallas_call x1, Pallas kernels, per_device(): pl.pallas_call(functools.partial(exchange, count_x, count_y), out_shape=(...  13 us
    pallas_call x1, Pallas kernels, per_device(): pl.pallas_call(finish, out_shape=(pltpu.HBM(adjoint_e.shape, bf16), pltpu...  1.7 us

profile of v5, /device:TPU:0, one launch (start us, length us, event | category | flops | bytes accessed | tf_op | source)
XLA Modules:
  0.0 15.4 jit_solution(4445195331965733427)
XLA Ops:
  0.6 13.0 %shard_map.103 = (bf16[3,32,64,128]{3,2,1,0:T(8,128)(2,1)S(1)}, bf16[3,32,64,128]{3,2,1,0:T(8,128)(2,1)S(1)}, f32[256,128]{1,0:T(8,128)S(1)}) custom-call(bf16[3,32,64,128]{3,2,1,0:T(8,128)(2,1)} %e_hbm.1, bf16[3,32,64,128]{3,2,1,0:T(8,128)(2,1)} %h_hbm.1, s32[32,64,128]{2,1,0:T(8,128)} %m_hbm.1, f32[4]{0:T(128)} %eps_hbm.1, bf16[3,32,64,128]{3,2,1,0:T(8,128)(2,1)} %f_hbm.1, ...), custom_call_target="tpu_custom_call" | custom-call | tf_op jit(solution)/shard_map/pallas_call | solution.py:502
  13.7 1.7 %shard_map.104 = (bf16[3,32,64,128]{3,2,1,0:T(8,128)(2,1)}, bf16[3,32,64,128]{3,2,1,0:T(8,128)(2,1)}, f32[32,512]{1,0:T(8,128)}) custom-call(bf16[3,32,64,128]{3,2,1,0:T(8,128)(2,1)S(1)} %get-tuple-element.6.ne_v, bf16[3,32,64,128]{3,2,1,0:T(8,128)(2,1)S(1)} %get-tuple-element.7.nh_v, f32[256,128]{1,0:T(8,128)S(1)} %get-tuple-element.8.recv), custom_call_target="tpu_custom_call" | custom-call | tf_op jit(solution)/shard_map/pallas_call | solution.py:545

commit v6 on v5

--- a/solution.py
+++ b/solution.py
@@ -119,23 +119,34 @@
     gx, gy = lax.axis_index("gx"), lax.axis_index("gy")
     me = gx * count_y + gy
 
+    def field(src, dst):
+        return [(src.at[c], dst.at[c, pl.ds(0, cx)]) for c in range(3)]
+
+    my_ranks = pr_hbm.at[pl.ds(pl.multiple_of(gx * rank_rows, 8), rank_rows)]
+    sources = [
+        [(tp_hbm.at[gx], tp_v)],
+        [(my_ranks, pr_v)],
+        field(e_hbm, e_v),
+        field(h_hbm, h_v),
+        [(cs_hbm, cs_v)],
+        field(f_hbm, f_v),
+        [(eps_hbm, eps_v)],
+        [(m_hbm, m_v)],
+    ]
     loads = [
-        pltpu.make_async_copy(src, dst, load_sem.at[i])
-        for i, (src, dst) in enumerate(
-            [
-                (tp_hbm.at[gx], tp_v),
-                (pr_hbm.at[pl.ds(pl.multiple_of(gx * rank_rows, 8), rank_rows)], pr_v),
-                (e_hbm, e_v.at[:, pl.ds(0, cx)]),
-                (h_hbm, h_v),
-                (cs_hbm, cs_v),
-                (f_hbm, f_v),
-                (eps_hbm, eps_v),
-                (m_hbm, m_v),
-            ]
-        )
+        [
+            pltpu.make_async_copy(src, dst, load_sem.at[3 * i + c])
+            for c, (src, dst) in enumerate(group)
+        ]
+        for i, group in enumerate(sources)
     ]
-    for load in loads:
-        load.start()
+    for i in (0, 1, 4, 2, 5, 3, 6, 7):
+        for load in loads[i]:
+            load.start()
+
+    def await_load(i):
+        for load in loads[i]:
+            load.wait()
 
     barrier = pltpu.get_barrier_semaphore()
 
@@ -155,8 +166,8 @@
 
     each_partner(greet)
 
-    loads[0].wait()
-    loads[1].wait()
+    await_load(0)
+    await_load(1)
     tile_row = iota(tp_v.shape, 0) == gy
     ids = jnp.sum(jnp.where(tile_row, tp_v[...], 0), axis=0, keepdims=True)
     listed = ids >= 0
@@ -206,9 +217,9 @@
         part = rank_lines[k * devices : (k + 1) * devices]
         rank_block = jnp.where(lane == k, part, rank_block)
 
-    loads[2].wait()
-    loads[4].wait()
-    loads[5].wait()
+    await_load(2)
+    await_load(4)
+    await_load(5)
     batch = 256 // cy
 
     def add_cells(g, carry):
@@ -227,7 +238,7 @@
 
     acc[...] = jnp.zeros_like(acc)
     lax.fori_loop(0, cx // batch, add_cells, 0, unroll=4)
-    loads[3].wait()
+    await_load(3)
 
     def gather_rows(x, carry):
         for c in range(3):
@@ -372,8 +383,8 @@
     hy_edge[0] = jnp.where(keep_y, edge_x, 0.0).astype(bf16).astype(f32)
     hy_edge[1] = jnp.where(keep_y, edge_z, 0.0).astype(bf16).astype(f32)
 
-    loads[6].wait()
-    loads[7].wait()
+    await_load(6)
+    await_load(7)
     materials = eps_v.shape[0]
     factors = [courant * eps_v[k] for k in range(materials)]
 
@@ -446,12 +457,13 @@
     groups = LANES // DL
     rows = owned // devices // groups
 
+    pairs = [(src.at[c], dst.at[c]) for src, dst in ((ne_v, ne), (nh_v, nh)) for c in range(3)]
     stores = [
         pltpu.make_async_copy(src, dst, store_sem.at[i])
-        for i, (src, dst) in enumerate([(ne_v, ne), (nh_v, nh), (grad_v, grad)])
+        for i, (src, dst) in enumerate(pairs + [(grad_v, grad)])
     ]
-    stores[0].start()
-    stores[1].start()
+    for store in stores[:-1]:
+        store.start()
 
     values = jnp.concatenate(
         [recv[pl.ds(i, devices, stride=BLOCK), :] for i in range(rows)], axis=0
@@ -469,7 +481,7 @@
     result = dot(jnp.concatenate(split(terms), axis=0), target)
     grad_v[...] = grad_scale * (result[:DL] + result[DL:])
 
-    stores[2].start()
+    stores[-1].start()
     for store in stores:
         store.wait()
 
@@ -532,7 +544,7 @@
             pltpu.VMEM((16, nz), bf16),
             pltpu.VMEM((2, cx, nz), f32),
             pltpu.VMEM((devices * BLOCK, LANES), f32),
-            pltpu.SemaphoreType.DMA((8,)),
+            pltpu.SemaphoreType.DMA((24,)),
             pltpu.SemaphoreType.DMA((7,)),
             pltpu.SemaphoreType.DMA((7,)),
             pltpu.SemaphoreType.DMA,
@@ -553,7 +565,7 @@
         out_specs=(anywhere,) * 3,
         scratch_shapes=[
             pltpu.VMEM((DL, owned), f32),
-            pltpu.SemaphoreType.DMA((3,)),
+            pltpu.SemaphoreType.DMA((7,)),
         ],
         compiler_params=pltpu.CompilerParams(vmem_limit_bytes=16 * 1024 * 1024),
     )(*[pltpu.with_memory_space_constraint(value, pltpu.VMEM) for value in kept])

time: 15.6 us -> 15.4 us (0.987)
  Pallas kernels: 14.7 us -> 14.5 us
    pallas_call x1, Pallas kernels: 13 us -> 12.8 us  [per_device(): pl.pallas_call(functools.partial(exchange, count_x, count_y), out_shape=(...]
where the time goes in v6:
time: 15.4 us; the launch traced here: 15.1 us
  Pallas kernels  14.5 us (94%)
  between operations  0.64 us (4%)
    pallas_call x1, Pallas kernels, per_device(): pl.pallas_call(functools.partial(exchange, count_x, count_y), out_shape=(...  12.8 us
    pallas_call x1, Pallas kernels, per_device(): pl.pallas_call(finish, out_shape=(pltpu.HBM(adjoint_e.shape, bf16), pltpu...  1.73 us

profile of v6, /device:TPU:0, one launch (start us, length us, event | category | flops | bytes accessed | tf_op | source)
XLA Modules:
  0.0 15.1 jit_solution(18013793283383410793)
XLA Ops:
  0.6 12.8 %shard_map.103 = (bf16[3,32,64,128]{3,2,1,0:T(8,128)(2,1)S(1)}, bf16[3,32,64,128]{3,2,1,0:T(8,128)(2,1)S(1)}, f32[256,128]{1,0:T(8,128)S(1)}) custom-call(bf16[3,32,64,128]{3,2,1,0:T(8,128)(2,1)} %e_hbm.1, bf16[3,32,64,128]{3,2,1,0:T(8,128)(2,1)} %h_hbm.1, s32[32,64,128]{2,1,0:T(8,128)} %m_hbm.1, f32[4]{0:T(128)} %eps_hbm.1, bf16[3,32,64,128]{3,2,1,0:T(8,128)(2,1)} %f_hbm.1, ...), custom_call_target="tpu_custom_call" | custom-call | tf_op jit(solution)/shard_map/pallas_call | solution.py:514
  13.4 1.7 %shard_map.104 = (bf16[3,32,64,128]{3,2,1,0:T(8,128)(2,1)}, bf16[3,32,64,128]{3,2,1,0:T(8,128)(2,1)}, f32[32,512]{1,0:T(8,128)}) custom-call(bf16[3,32,64,128]{3,2,1,0:T(8,128)(2,1)S(1)} %get-tuple-element.6.ne_v, bf16[3,32,64,128]{3,2,1,0:T(8,128)(2,1)S(1)} %get-tuple-element.7.nh_v, f32[256,128]{1,0:T(8,128)S(1)} %get-tuple-element.8.recv), custom_call_target="tpu_custom_call" | custom-call | tf_op jit(solution)/shard_map/pallas_call | solution.py:557
